TPU v7x, 512 devices: a whole 4x8x8 slice. The times are simulated.
512 devices in a mesh: ctx: 64 (over z, x, core), head: 8 (over y).
Axes of the slice: x: 4, y: 8, z: 8, core: 2. Of those that a mesh axis runs over, the one named last changes fastest.
Arguments:
- queries: bfloat16 [8192, 8192], P('ctx', 'head'), may hold values from -6 to 6
- keys: bfloat16 [8192, 1024], P(('ctx', 'head')), may hold values from -6 to 6
- values: bfloat16 [8192, 1024], P(('ctx', 'head')), may hold values from -6 to 6
- output_gradient: bfloat16 [8192, 8192], P('ctx', 'head'), may hold values from -6 to 6
- doc_lengths: int32 [128], replicated, may hold values from 1 to 640, 8192 in all
Outputs:
- attended: bfloat16 [8192, 8192], P('ctx', 'head')
- grad_queries: bfloat16 [8192, 8192], P('ctx', 'head')
- key_gradient: bfloat16 [8192, 1024], P(('ctx', 'head'))
- value_gradient: bfloat16 [8192, 1024], P(('ctx', 'head'))
Inputs may be any that keep to these rules, and one draw needn't show every extreme that they name: `doc_lengths`: the lengths sum to 8192; the longest is exactly 640.
All inputs are finite; a program needn't handle non-finite values.
Results may differ from a plain program's by a relative error of at most 0.03.
Values may be sent and summed in bfloat16 or wider, within the bound.
A program may use at most 64 MiB of HBM per device.

v0:
```python
import jax
import jax.numpy as jnp
from jax import lax
from jax.sharding import PartitionSpec as P

HEAD_SIZE = 128
SPAN = 5


big_negative = -1e30


def passed_along(block, axis, distance):
    devices = range(lax.axis_size(axis))
    route = [(i - distance, i) for i in devices if i - distance in devices]
    return lax.ppermute(block, axis, route)


def document_ids(doc_lengths, positions):
    ends = jnp.cumsum(doc_lengths)
    return jnp.sum((positions[:, None] >= ends[None, :]).astype(jnp.int32), axis=1)


def masked_scores(q_block, k_block, q_docs, k_docs, same_block, scale):
    scores = (
        jnp.einsum("rghd,kgd->ghrk", q_block, k_block, preferred_element_type=jnp.float32) * scale
    )
    visible = q_docs[:, None] == k_docs[None, :]
    if same_block:
        places = jnp.arange(q_docs.shape[0], dtype=jnp.int32)
        visible = visible & (places[None, :] <= places[:, None])
    return jnp.where(visible[None, None], scores, big_negative)


def per_device(queries, keys, values, output_gradient, doc_lengths):
    rows = queries.shape[0]
    scale = HEAD_SIZE ** (-0.5)
    k_local, v_local = (
        lax.all_to_all(keys, "head", split_axis=1, concat_axis=0, tiled=True),
        lax.all_to_all(values, "head", split_axis=1, concat_axis=0, tiled=True),
    )
    kv_groups = k_local.shape[1] // HEAD_SIZE
    head_group = queries.shape[1] // HEAD_SIZE // kv_groups
    k_own = k_local.reshape(rows, kv_groups, HEAD_SIZE)
    v_own = v_local.reshape(rows, kv_groups, HEAD_SIZE)
    q_own = queries.reshape(rows, kv_groups, head_group, HEAD_SIZE)
    g_own = output_gradient.reshape(rows, kv_groups, head_group, HEAD_SIZE)
    me = lax.axis_index("ctx")
    offsets_row = jnp.arange(rows, dtype=jnp.int32)
    q_docs = document_ids(doc_lengths, me * rows + offsets_row)
    k_list = [k_own]
    v_list = [v_own]
    for offset in range(1, SPAN + 1):
        k_far, v_far = passed_along((k_own, v_own), "ctx", offset)
        k_list.append(k_far)
        v_list.append(v_far)
    k_stack = jnp.stack(k_list)
    v_stack = jnp.stack(v_list)
    k_docs = [
        document_ids(doc_lengths, (me - offset) * rows + offsets_row) for offset in range(SPAN + 1)
    ]
    live = [
        (me - offset >= 0) & (k_docs[offset][rows - 1] == q_docs[0]) for offset in range(SPAN + 1)
    ]
    tile_shape = (kv_groups, head_group, rows, rows)
    score_tiles = [masked_scores(q_own, k_stack[0], q_docs, k_docs[0], True, scale)]
    for offset in range(1, SPAN + 1):

        def live_scores(offset=offset):
            return masked_scores(q_own, k_stack[offset], q_docs, k_docs[offset], False, scale)

        def dead_scores():
            return jnp.full(tile_shape, big_negative, jnp.float32)

        score_tiles.append(lax.cond(live[offset], live_scores, dead_scores))
    top = jnp.max(score_tiles[0], axis=3)
    total = jnp.sum(jnp.exp(score_tiles[0] - top[..., None]), axis=3)
    for offset in range(1, SPAN + 1):

        def widen(carry, offset=offset):
            old_top, old_total = carry
            scores = score_tiles[offset]
            new_top = jnp.maximum(old_top, jnp.max(scores, axis=3))
            grown = old_total * jnp.exp(old_top - new_top) + jnp.sum(
                jnp.exp(scores - new_top[..., None]), axis=3
            )
            return (new_top, grown)

        top, total = lax.cond(live[offset], widen, lambda carry: carry, (top, total))
    lse = top + jnp.log(total)
    prob_tiles = [jnp.exp(score_tiles[0] - lse[..., None]).astype(jnp.bfloat16)]
    for offset in range(1, SPAN + 1):

        def live_probs(offset=offset):
            return jnp.exp(score_tiles[offset] - lse[..., None]).astype(jnp.bfloat16)

        def dead_probs():
            return jnp.zeros(tile_shape, jnp.bfloat16)

        prob_tiles.append(lax.cond(live[offset], live_probs, dead_probs))
    output_acc = jnp.einsum(
        "ghrk,kgd->rghd", prob_tiles[0], v_stack[0], preferred_element_type=jnp.float32
    )
    for offset in range(1, SPAN + 1):

        def add_output(acc, offset=offset):
            return acc + jnp.einsum(
                "ghrk,kgd->rghd",
                prob_tiles[offset],
                v_stack[offset],
                preferred_element_type=jnp.float32,
            )

        output_acc = lax.cond(live[offset], add_output, lambda acc: acc, output_acc)
    attended = output_acc.astype(jnp.bfloat16)
    delta = jnp.sum(g_own.astype(jnp.float32) * attended.astype(jnp.float32), axis=3).transpose(
        1, 2, 0
    )

    def tile_grads(offset):
        probs = prob_tiles[offset]
        dprobs = jnp.einsum(
            "rghd,kgd->ghrk", g_own, v_stack[offset], preferred_element_type=jnp.float32
        )
        dscores = (probs.astype(jnp.float32) * (dprobs - delta[..., None]) * scale).astype(
            jnp.bfloat16
        )
        dq_part = jnp.einsum(
            "ghrk,kgd->rghd", dscores, k_stack[offset], preferred_element_type=jnp.float32
        )
        dk_part = jnp.einsum("ghrk,rghd->kgd", dscores, q_own, preferred_element_type=jnp.float32)
        dv_part = jnp.einsum("ghrk,rghd->kgd", probs, g_own, preferred_element_type=jnp.float32)
        return (dq_part, dk_part, dv_part)

    dq_acc, dk_first, dv_first = tile_grads(0)
    dk_parts = [dk_first]
    dv_parts = [dv_first]
    zero_part = jnp.zeros((rows, kv_groups, HEAD_SIZE), jnp.float32)
    for offset in range(1, SPAN + 1):

        def grads_live(acc, offset=offset):
            dq_part, dk_part, dv_part = tile_grads(offset)
            return (acc + dq_part, dk_part, dv_part)

        def grads_dead(acc):
            return (acc, zero_part, zero_part)

        dq_acc, dk_part, dv_part = lax.cond(live[offset], grads_live, grads_dead, dq_acc)
        dk_parts.append(dk_part)
        dv_parts.append(dv_part)
    dk_stack = jnp.stack(dk_parts)
    dv_stack = jnp.stack(dv_parts)
    dk_total = dk_stack[0]
    dv_total = dv_stack[0]
    for offset in range(1, SPAN + 1):
        dk_back, dv_back = passed_along((dk_stack[offset], dv_stack[offset]), "ctx", -offset)
        dk_total = dk_total + dk_back
        dv_total = dv_total + dv_back
    grad_k = dk_total.astype(jnp.bfloat16).reshape(rows, kv_groups * HEAD_SIZE)
    grad_v = dv_total.astype(jnp.bfloat16).reshape(rows, kv_groups * HEAD_SIZE)
    key_gradient, value_gradient = (
        lax.all_to_all(grad_k, "head", split_axis=0, concat_axis=1, tiled=True),
        lax.all_to_all(grad_v, "head", split_axis=0, concat_axis=1, tiled=True),
    )
    attended_out = attended.reshape(rows, kv_groups * head_group * HEAD_SIZE)
    grad_queries = dq_acc.astype(jnp.bfloat16).reshape(rows, kv_groups * head_group * HEAD_SIZE)
    return (attended_out, grad_queries, key_gradient, value_gradient)


def solution(mesh):
    return jax.shard_map(
        per_device,
        mesh=mesh,
        in_specs=(
            P("ctx", "head"),
            P(("ctx", "head"), None),
            P(("ctx", "head"), None),
            P("ctx", "head"),
            P(),
        ),
        out_specs=(
            P("ctx", "head"),
            P("ctx", "head"),
            P(("ctx", "head"), None),
            P(("ctx", "head"), None),
        ),
        check_vma=False,
    )
```

profile of v0, /device:TPU:320, one launch (start us, length us, event | category | flops | bytes accessed | tf_op | source)
XLA Modules:
  0.0 162.4 jit_solution(5677088250982803821)
XLA Ops:
  2.0 7.2 %all-to-all-start = ((bf16[16,8,128]{2,0,1:T(8,128)(2,1)}), bf16[16,8,128]{2,0,1:T(8,128)(2,1)S(1)}, u32[]{:S(2)}, u32[]{:S(2)}) async-start(bf16[16,8,128]{2,0,1:T(8,128)(2,1)} %copy_bitcast_fusion.4), calls=%async_computation | async-start | bytes 65536 | tf_op jit(solution)/shard_map/all_to_all | solution.py:39
  18.0 7.2 %all-to-all-start.1 = ((bf16[16,8,128]{2,0,1:T(8,128)(2,1)}), bf16[16,8,128]{2,0,1:T(8,128)(2,1)S(1)}, u32[]{:S(2)}, u32[]{:S(2)}) async-start(bf16[16,8,128]{2,0,1:T(8,128)(2,1)} %copy_bitcast_fusion.3), calls=%async_computation.1 | async-start | bytes 65536 | tf_op jit(solution)/shard_map/all_to_all | solution.py:40
  25.2 1.9 %collective-permute-start = (bf16[128,1,128]{2,0,1:T(8,128)(2,1)S(1)}, bf16[128,1,128]{2,0,1:T(8,128)(2,1)S(1)}, u32[]{:S(2)}, u32[]{:S(2)}) collective-permute-start(bf16[128,1,128]{2,0,1:T(8,128)(2,1)S(1)} %bitcast.650), channel_id=1, source_target_pairs={{0,8},{8,16},{16,24},{24,32},{32,40},{40,48},{48,56},{56,64},{64,7... | collective-permute-start | bytes 98312 | tf_op jit(solution)/shard_map/ppermute | solution.py:16
  27.1 3.4 %collective-permute-start.1 = (bf16[128,1,128]{2,0,1:T(8,128)(2,1)S(1)}, bf16[128,1,128]{2,0,1:T(8,128)(2,1)S(1)}, u32[]{:S(2)}, u32[]{:S(2)}) collective-permute-start(bf16[128,1,128]{2,0,1:T(8,128)(2,1)S(1)} %bitcast.651), channel_id=1, source_target_pairs={{0,16},{8,24},{16,32},{24,40},{32,48},{40,56},{48,64},{56,72},{64,... | collective-permute-start | bytes 98312 | tf_op jit(solution)/shard_map/ppermute | solution.py:16
  30.5 4.0 %collective-permute-start.2 = (bf16[128,1,128]{2,0,1:T(8,128)(2,1)S(1)}, bf16[128,1,128]{2,0,1:T(8,128)(2,1)S(1)}, u32[]{:S(2)}, u32[]{:S(2)}) collective-permute-start(bf16[128,1,128]{2,0,1:T(8,128)(2,1)S(1)} %bitcast.652), channel_id=1, source_target_pairs={{0,24},{8,32},{16,40},{24,48},{32,56},{40,64},{48,72},{56,80},{64,... | collective-permute-start | bytes 98312 | tf_op jit(solution)/shard_map/ppermute | solution.py:16
  34.5 4.8 %collective-permute-start.3 = (bf16[128,1,128]{2,0,1:T(8,128)(2,1)S(1)}, bf16[128,1,128]{2,0,1:T(8,128)(2,1)S(1)}, u32[]{:S(2)}, u32[]{:S(2)}) collective-permute-start(bf16[128,1,128]{2,0,1:T(8,128)(2,1)S(1)} %bitcast.653), channel_id=1, source_target_pairs={{0,32},{8,40},{16,48},{24,56},{32,64},{40,72},{48,80},{56,88},{64,... | collective-permute-start | bytes 98312 | tf_op jit(solution)/shard_map/ppermute | solution.py:16
  39.4 3.5 %collective-permute-start.4 = (bf16[128,1,128]{2,0,1:T(8,128)(2,1)S(1)}, bf16[128,1,128]{2,0,1:T(8,128)(2,1)S(1)}, u32[]{:S(2)}, u32[]{:S(2)}) collective-permute-start(bf16[128,1,128]{2,0,1:T(8,128)(2,1)S(1)} %bitcast.654), channel_id=1, source_target_pairs={{0,40},{8,48},{16,56},{24,64},{32,72},{40,80},{48,88},{56,96},{64,... | collective-permute-start | bytes 98312 | tf_op jit(solution)/shard_map/ppermute | solution.py:16
  44.0 2.5 %collective-permute-start.5 = (bf16[128,1,128]{2,0,1:T(8,128)(2,1)S(1)}, bf16[128,1,128]{2,0,1:T(8,128)(2,1)}, u32[]{:S(2)}, u32[]{:S(2)}) collective-permute-start(bf16[128,1,128]{2,0,1:T(8,128)(2,1)S(1)} %bitcast.657), channel_id=1, source_target_pairs={{0,8},{8,16},{16,24},{24,32},{32,40},{40,48},{48,56},{56,64},{64,7... | collective-permute-start | bytes 98312 | tf_op jit(solution)/shard_map/ppermute | solution.py:16
  47.6 2.8 %collective-permute-start.6 = (bf16[128,1,128]{2,0,1:T(8,128)(2,1)S(1)}, bf16[128,1,128]{2,0,1:T(8,128)(2,1)}, u32[]{:S(2)}, u32[]{:S(2)}) collective-permute-start(bf16[128,1,128]{2,0,1:T(8,128)(2,1)S(1)} %bitcast.658), channel_id=1, source_target_pairs={{0,16},{8,24},{16,32},{24,40},{32,48},{40,56},{48,64},{56,72},{64,... | collective-permute-start | bytes 98312 | tf_op jit(solution)/shard_map/ppermute | solution.py:16
  50.5 3.6 %collective-permute-start.7 = (bf16[128,1,128]{2,0,1:T(8,128)(2,1)S(1)}, bf16[128,1,128]{2,0,1:T(8,128)(2,1)}, u32[]{:S(2)}, u32[]{:S(2)}) collective-permute-start(bf16[128,1,128]{2,0,1:T(8,128)(2,1)S(1)} %bitcast.659), channel_id=1, source_target_pairs={{0,24},{8,32},{16,40},{24,48},{32,56},{40,64},{48,72},{56,80},{64,... | collective-permute-start | bytes 98312 | tf_op jit(solution)/shard_map/ppermute | solution.py:16
  54.3 5.0 %collective-permute-start.8 = (bf16[128,1,128]{2,0,1:T(8,128)(2,1)S(1)}, bf16[128,1,128]{2,0,1:T(8,128)(2,1)}, u32[]{:S(2)}, u32[]{:S(2)}) collective-permute-start(bf16[128,1,128]{2,0,1:T(8,128)(2,1)S(1)} %bitcast.660), channel_id=1, source_target_pairs={{0,32},{8,40},{16,48},{24,56},{32,64},{40,72},{48,80},{56,88},{64,... | collective-permute-start | bytes 98312 | tf_op jit(solution)/shard_map/ppermute | solution.py:16
  59.4 1.9 %collective-permute-start.9 = (bf16[128,1,128]{2,0,1:T(8,128)(2,1)S(1)}, bf16[128,1,128]{2,0,1:T(8,128)(2,1)S(1)}, u32[]{:S(2)}, u32[]{:S(2)}) collective-permute-start(bf16[128,1,128]{2,0,1:T(8,128)(2,1)S(1)} %bitcast.661), channel_id=1, source_target_pairs={{0,40},{8,48},{16,56},{24,64},{32,72},{40,80},{48,88},{56,96},{64,... | collective-permute-start | bytes 98312 | tf_op jit(solution)/shard_map/ppermute | solution.py:16
  65.3 3.0 %conditional.40 = (bf16[1,8,128,128]{3,2,1,0:T(8,128)(2,1)}) conditional(s32[]{:T(128)} %convert_element_type.157, () %tuple.202, (f32[1,8,128]{2,1,0:T(8,128)S(1)}, f32[1,8,128,128]{2,3,1,0:T(8,128)S(1)}) %tuple.203), branch_computations={%region_39.40_spmd, %region_40.41_spmd} | conditional | flops 262144 | bytes 1839112 | solution.py:100
  66.3 2.0 %exponential_convert_fusion = bf16[1,8,128,128]{3,2,1,0:T(8,128)(2,1)} fusion(f32[1,8,128,128]{3,2,1,0:T(8,128)} %copy.178, f32[8,128]{1,0:T(8,128)S(1)} %bitcast.678), kind=kLoop, calls=%fused_computation.45 | loop fusion | flops 262144 | bytes 790528 | tf_op jit(solution)/shard_map/cond/branch_1_fun/convert_element_type | solution.py:95
  68.2 2.4 %conditional.41 = (f32[128,1,8,128]{0,3,2,1:T(8,128)S(1)}) conditional(s32[]{:T(128)} %convert_element_type.157, (f32[128,1,8,128]{3,0,2,1:T(8,128)S(1)}) %tuple.414, (bf16[128,1,128]{2,0,1:T(8,128)(2,1)}, bf16[1,8,128,128]{3,2,1,0:T(8,128)(2,1)}, f32[128,1,8,128]{3,0,2,1:T(8,128)S(1)}) %tuple.415), branch_computations={%region_41.42_spmd, %region_42.43_spmd} | conditional | flops 33685504 | bytes 2392072 | solution.py:114
  69.2 1.4 fusion.20
  73.2 3.9 %conditional.50 = (f32[128,1,8,128]{3,0,2,1:T(8,128)S(1)}, f32[128,1,128]{2,0,1:T(8,128)S(1)}, f32[128,1,128]{2,0,1:T(8,128)S(1)}) conditional(s32[]{:T(128)} %convert_element_type.157, f32[128,1,8,128]{3,0,2,1:T(8,128)S(1)} %convolution_bitcast_fusion.25, (bf16[1,8,128,128]{3,2,1,0:T(8,128)(2,1)}, bf16[128,1,128]{2,0,1:T(8,128)(2,1)}, ...), branch_computations={%region_60.61_spmd, %region_61.62_spmd} | conditional | flops 135004160 | bytes 4001816 | solution.py:148
  75.9 1.2 convolution_bitcast_fusion.7
  79.5 4.7 %collective-permute-start.19 = (f32[128,1,128]{2,0,1:T(8,128)S(1)}, f32[128,1,128]{2,0,1:T(8,128)S(1)}, u32[]{:S(2)}, u32[]{:S(2)}) collective-permute-start(f32[128,1,128]{2,0,1:T(8,128)S(1)} %get-tuple-element.766), channel_id=1, source_target_pairs={{40,0},{48,8},{56,16},{64,24},{72,32},{80,40},{88,48},{96,56},{104... | collective-permute-start | bytes 196616 | tf_op jit(solution)/shard_map/ppermute | solution.py:16
  84.1 16.6 %collective-permute-start.18 = (f32[128,1,128]{2,0,1:T(8,128)S(1)}, f32[128,1,128]{2,0,1:T(8,128)S(1)}, u32[]{:S(2)}, u32[]{:S(2)}) collective-permute-start(f32[128,1,128]{2,0,1:T(8,128)S(1)} %get-tuple-element.765), channel_id=1, source_target_pairs={{32,0},{40,8},{48,16},{56,24},{64,32},{72,40},{80,48},{88,56},{96,... | collective-permute-start | bytes 196616 | tf_op jit(solution)/shard_map/ppermute | solution.py:16
  100.7 5.2 %collective-permute-start.17 = (f32[128,1,128]{2,0,1:T(8,128)S(1)}, f32[128,1,128]{2,0,1:T(8,128)S(1)}, u32[]{:S(2)}, u32[]{:S(2)}) collective-permute-start(f32[128,1,128]{2,0,1:T(8,128)S(1)} %get-tuple-element.764), channel_id=1, source_target_pairs={{24,0},{32,8},{40,16},{48,24},{56,32},{64,40},{72,48},{80,56},{88,... | collective-permute-start | bytes 196616 | tf_op jit(solution)/shard_map/ppermute | solution.py:16
  105.9 1.9 %collective-permute-start.16 = (f32[128,1,128]{2,0,1:T(8,128)S(1)}, f32[128,1,128]{2,0,1:T(8,128)S(1)}, u32[]{:S(2)}, u32[]{:S(2)}) collective-permute-start(f32[128,1,128]{2,0,1:T(8,128)S(1)} %get-tuple-element.763), channel_id=1, source_target_pairs={{16,0},{24,8},{32,16},{40,24},{48,32},{56,40},{64,48},{72,56},{80,... | collective-permute-start | bytes 196616 | tf_op jit(solution)/shard_map/ppermute | solution.py:16
  107.9 2.5 %collective-permute-start.15 = (f32[128,1,128]{2,0,1:T(8,128)S(1)}, f32[128,1,128]{2,0,1:T(8,128)S(1)}, u32[]{:S(2)}, u32[]{:S(2)}) collective-permute-start(f32[128,1,128]{2,0,1:T(8,128)S(1)} %get-tuple-element.762), channel_id=1, source_target_pairs={{8,0},{16,8},{24,16},{32,24},{40,32},{48,40},{56,48},{64,56},{72,6... | collective-permute-start | bytes 196616 | tf_op jit(solution)/shard_map/ppermute | solution.py:16
  111.6 1.9 %collective-permute-start.14 = (f32[128,1,128]{2,0,1:T(8,128)S(1)}, f32[128,1,128]{2,0,1:T(8,128)S(1)}, u32[]{:S(2)}, u32[]{:S(2)}) collective-permute-start(f32[128,1,128]{2,0,1:T(8,128)S(1)} %get-tuple-element.426), channel_id=1, source_target_pairs={{40,0},{48,8},{56,16},{64,24},{72,32},{80,40},{88,48},{96,56},{104... | collective-permute-start | bytes 196616 | tf_op jit(solution)/shard_map/ppermute | solution.py:16
  113.5 12.0 %collective-permute-start.13 = (f32[128,1,128]{2,0,1:T(8,128)S(1)}, f32[128,1,128]{2,0,1:T(8,128)S(1)}, u32[]{:S(2)}, u32[]{:S(2)}) collective-permute-start(f32[128,1,128]{2,0,1:T(8,128)S(1)} %get-tuple-element.425), channel_id=1, source_target_pairs={{32,0},{40,8},{48,16},{56,24},{64,32},{72,40},{80,48},{88,56},{96,... | collective-permute-start | bytes 196616 | tf_op jit(solution)/shard_map/ppermute | solution.py:16
  125.5 4.0 %collective-permute-start.12 = (f32[128,1,128]{2,0,1:T(8,128)S(1)}, f32[128,1,128]{2,0,1:T(8,128)S(1)}, u32[]{:S(2)}, u32[]{:S(2)}) collective-permute-start(f32[128,1,128]{2,0,1:T(8,128)S(1)} %get-tuple-element.424), channel_id=1, source_target_pairs={{24,0},{32,8},{40,16},{48,24},{56,32},{64,40},{72,48},{80,56},{88,... | collective-permute-start | bytes 196616 | tf_op jit(solution)/shard_map/ppermute | solution.py:16
  129.6 3.1 %collective-permute-start.11 = (f32[128,1,128]{2,0,1:T(8,128)S(1)}, f32[128,1,128]{2,0,1:T(8,128)S(1)}, u32[]{:S(2)}, u32[]{:S(2)}) collective-permute-start(f32[128,1,128]{2,0,1:T(8,128)S(1)} %get-tuple-element.423), channel_id=1, source_target_pairs={{16,0},{24,8},{32,16},{40,24},{48,32},{56,40},{64,48},{72,56},{80,... | collective-permute-start | bytes 196616 | tf_op jit(solution)/shard_map/ppermute | solution.py:16
  132.7 1.9 %collective-permute-start.10 = (f32[128,1,128]{2,0,1:T(8,128)S(1)}, f32[128,1,128]{2,0,1:T(8,128)S(1)}, u32[]{:S(2)}, u32[]{:S(2)}) collective-permute-start(f32[128,1,128]{2,0,1:T(8,128)S(1)} %get-tuple-element.422), channel_id=1, source_target_pairs={{8,0},{16,8},{24,16},{32,24},{40,32},{48,40},{56,48},{64,56},{72,6... | collective-permute-start | bytes 196616 | tf_op jit(solution)/shard_map/ppermute | solution.py:16
  135.2 7.2 %all-to-all-start.3 = ((bf16[8,16,128]{2,1,0:T(8,128)(2,1)}), bf16[8,16,128]{2,1,0:T(8,128)(2,1)S(1)}, u32[]{:S(2)}, u32[]{:S(2)}) async-start(bf16[8,16,128]{2,1,0:T(8,128)(2,1)} %bitcast.237), calls=%async_computation.3 | async-start | bytes 65536 | tf_op jit(solution)/shard_map/all_to_all | solution.py:163
  143.1 7.3 %all-to-all-done.3 = bf16[8,16,128]{2,1,0:T(8,128)(2,1)S(1)} async-done(((bf16[8,16,128]{2,1,0:T(8,128)(2,1)}), bf16[8,16,128]{2,1,0:T(8,128)(2,1)S(1)}, u32[]{:S(2)}, u32[]{:S(2)}) %all-to-all-start.3) | async-done | bytes 32800 | tf_op jit(solution)/shard_map/all_to_all | solution.py:163
  150.5 3.3 %all-to-all-start.2 = ((bf16[8,16,128]{2,1,0:T(8,128)(2,1)}), bf16[8,16,128]{2,1,0:T(8,128)(2,1)S(1)}, u32[]{:S(2)}, u32[]{:S(2)}) async-start(bf16[8,16,128]{2,1,0:T(8,128)(2,1)} %bitcast.231), calls=%async_computation.2 | async-start | bytes 65536 | tf_op jit(solution)/shard_map/all_to_all | solution.py:162
  154.4 7.3 %all-to-all-done.2 = bf16[8,16,128]{2,1,0:T(8,128)(2,1)S(1)} async-done(((bf16[8,16,128]{2,1,0:T(8,128)(2,1)}), bf16[8,16,128]{2,1,0:T(8,128)(2,1)S(1)}, u32[]{:S(2)}, u32[]{:S(2)}) %all-to-all-start.2) | async-done | bytes 32800 | tf_op jit(solution)/shard_map/all_to_all | solution.py:162
  (155 shorter events, 28.3 us)
Async XLA Ops:
  1.4 7.9 %copy-start.21 = (s32[128]{0:T(128)S(1)}, s32[128]{0:T(128)}, u32[]{:S(2)}) copy-start(s32[128]{0:T(128)} %param.59) | copy-start | bytes 1540
  2.0 9.3 %copy-start.6 = (bf16[128,1024]{1,0:T(8,128)(2,1)S(1)}, bf16[128,1024]{1,0:T(8,128)(2,1)}, u32[]{:S(2)}) copy-start(bf16[128,1024]{1,0:T(8,128)(2,1)} %param.55) | copy-start | bytes 786436
  2.0 15.9 %all-to-all-start = ((bf16[16,8,128]{2,0,1:T(8,128)(2,1)}), bf16[16,8,128]{2,0,1:T(8,128)(2,1)S(1)}, u32[]{:S(2)}, u32[]{:S(2)}) async-start(bf16[16,8,128]{2,0,1:T(8,128)(2,1)} %copy_bitcast_fusion.4), calls=%async_computation | async-start | bytes 65536 | tf_op jit(solution)/shard_map/all_to_all | solution.py:39
  11.4 6.4 %copy-start.3 = (bf16[128,1024]{1,0:T(8,128)(2,1)S(1)}, bf16[128,1024]{1,0:T(8,128)(2,1)}, u32[]{:S(2)}) copy-start(bf16[128,1024]{1,0:T(8,128)(2,1)} %param.58) | copy-start | bytes 786436
  18.0 26.0 %all-to-all-start.1 = ((bf16[16,8,128]{2,0,1:T(8,128)(2,1)}), bf16[16,8,128]{2,0,1:T(8,128)(2,1)S(1)}, u32[]{:S(2)}, u32[]{:S(2)}) async-start(bf16[16,8,128]{2,0,1:T(8,128)(2,1)} %copy_bitcast_fusion.3), calls=%async_computation.1 | async-start | bytes 65536 | tf_op jit(solution)/shard_map/all_to_all | solution.py:40
  25.2 18.8 %collective-permute-start = (bf16[128,1,128]{2,0,1:T(8,128)(2,1)S(1)}, bf16[128,1,128]{2,0,1:T(8,128)(2,1)S(1)}, u32[]{:S(2)}, u32[]{:S(2)}) collective-permute-start(bf16[128,1,128]{2,0,1:T(8,128)(2,1)S(1)} %bitcast.650), channel_id=1, source_target_pairs={{0,8},{8,16},{16,24},{24,32},{32,40},{40,48},{48,56},{56,64},{64,7... | collective-permute-start | bytes 98312 | tf_op jit(solution)/shard_map/ppermute | solution.py:16
  27.1 20.5 %collective-permute-start.1 = (bf16[128,1,128]{2,0,1:T(8,128)(2,1)S(1)}, bf16[128,1,128]{2,0,1:T(8,128)(2,1)S(1)}, u32[]{:S(2)}, u32[]{:S(2)}) collective-permute-start(bf16[128,1,128]{2,0,1:T(8,128)(2,1)S(1)} %bitcast.651), channel_id=1, source_target_pairs={{0,16},{8,24},{16,32},{24,40},{32,48},{40,56},{48,64},{56,72},{64,... | collective-permute-start | bytes 98312 | tf_op jit(solution)/shard_map/ppermute | solution.py:16
  30.5 20.0 %collective-permute-start.2 = (bf16[128,1,128]{2,0,1:T(8,128)(2,1)S(1)}, bf16[128,1,128]{2,0,1:T(8,128)(2,1)S(1)}, u32[]{:S(2)}, u32[]{:S(2)}) collective-permute-start(bf16[128,1,128]{2,0,1:T(8,128)(2,1)S(1)} %bitcast.652), channel_id=1, source_target_pairs={{0,24},{8,32},{16,40},{24,48},{32,56},{40,64},{48,72},{56,80},{64,... | collective-permute-start | bytes 98312 | tf_op jit(solution)/shard_map/ppermute | solution.py:16
  34.5 19.7 %collective-permute-start.3 = (bf16[128,1,128]{2,0,1:T(8,128)(2,1)S(1)}, bf16[128,1,128]{2,0,1:T(8,128)(2,1)S(1)}, u32[]{:S(2)}, u32[]{:S(2)}) collective-permute-start(bf16[128,1,128]{2,0,1:T(8,128)(2,1)S(1)} %bitcast.653), channel_id=1, source_target_pairs={{0,32},{8,40},{16,48},{24,56},{32,64},{40,72},{48,80},{56,88},{64,... | collective-permute-start | bytes 98312 | tf_op jit(solution)/shard_map/ppermute | solution.py:16
  39.4 20.0 %collective-permute-start.4 = (bf16[128,1,128]{2,0,1:T(8,128)(2,1)S(1)}, bf16[128,1,128]{2,0,1:T(8,128)(2,1)S(1)}, u32[]{:S(2)}, u32[]{:S(2)}) collective-permute-start(bf16[128,1,128]{2,0,1:T(8,128)(2,1)S(1)} %bitcast.654), channel_id=1, source_target_pairs={{0,40},{8,48},{16,56},{24,64},{32,72},{40,80},{48,88},{56,96},{64,... | collective-permute-start | bytes 98312 | tf_op jit(solution)/shard_map/ppermute | solution.py:16
  44.0 24.2 %collective-permute-start.5 = (bf16[128,1,128]{2,0,1:T(8,128)(2,1)S(1)}, bf16[128,1,128]{2,0,1:T(8,128)(2,1)}, u32[]{:S(2)}, u32[]{:S(2)}) collective-permute-start(bf16[128,1,128]{2,0,1:T(8,128)(2,1)S(1)} %bitcast.657), channel_id=1, source_target_pairs={{0,8},{8,16},{16,24},{24,32},{32,40},{40,48},{48,56},{56,64},{64,7... | collective-permute-start | bytes 98312 | tf_op jit(solution)/shard_map/ppermute | solution.py:16
  47.6 23.0 %collective-permute-start.6 = (bf16[128,1,128]{2,0,1:T(8,128)(2,1)S(1)}, bf16[128,1,128]{2,0,1:T(8,128)(2,1)}, u32[]{:S(2)}, u32[]{:S(2)}) collective-permute-start(bf16[128,1,128]{2,0,1:T(8,128)(2,1)S(1)} %bitcast.658), channel_id=1, source_target_pairs={{0,16},{8,24},{16,32},{24,40},{32,48},{40,56},{48,64},{56,72},{64,... | collective-permute-start | bytes 98312 | tf_op jit(solution)/shard_map/ppermute | solution.py:16
  50.5 3.7 %copy-start.14 = (bf16[128,1,128]{2,0,1:T(8,128)(2,1)}, bf16[128,1,128]{2,0,1:T(8,128)(2,1)S(1)}, u32[]{:S(2)}) copy-start(bf16[128,1,128]{2,0,1:T(8,128)(2,1)S(1)} %collective-permute-done.2) | copy-start | bytes 98308
  50.5 20.2 %collective-permute-start.7 = (bf16[128,1,128]{2,0,1:T(8,128)(2,1)S(1)}, bf16[128,1,128]{2,0,1:T(8,128)(2,1)}, u32[]{:S(2)}, u32[]{:S(2)}) collective-permute-start(bf16[128,1,128]{2,0,1:T(8,128)(2,1)S(1)} %bitcast.659), channel_id=1, source_target_pairs={{0,24},{8,32},{16,40},{24,48},{32,56},{40,64},{48,72},{56,80},{64,... | collective-permute-start | bytes 98312 | tf_op jit(solution)/shard_map/ppermute | solution.py:16
  54.3 5.0 %copy-start.12 = (bf16[128,1,128]{2,0,1:T(8,128)(2,1)}, bf16[128,1,128]{2,0,1:T(8,128)(2,1)S(1)}, u32[]{:S(2)}) copy-start(bf16[128,1,128]{2,0,1:T(8,128)(2,1)S(1)} %collective-permute-done.3) | copy-start | bytes 98308
  54.3 16.6 %collective-permute-start.8 = (bf16[128,1,128]{2,0,1:T(8,128)(2,1)S(1)}, bf16[128,1,128]{2,0,1:T(8,128)(2,1)}, u32[]{:S(2)}, u32[]{:S(2)}) collective-permute-start(bf16[128,1,128]{2,0,1:T(8,128)(2,1)S(1)} %bitcast.660), channel_id=1, source_target_pairs={{0,32},{8,40},{16,48},{24,56},{32,64},{40,72},{48,80},{56,88},{64,... | collective-permute-start | bytes 98312 | tf_op jit(solution)/shard_map/ppermute | solution.py:16
  59.4 11.5 %collective-permute-start.9 = (bf16[128,1,128]{2,0,1:T(8,128)(2,1)S(1)}, bf16[128,1,128]{2,0,1:T(8,128)(2,1)S(1)}, u32[]{:S(2)}, u32[]{:S(2)}) collective-permute-start(bf16[128,1,128]{2,0,1:T(8,128)(2,1)S(1)} %bitcast.661), channel_id=1, source_target_pairs={{0,40},{8,48},{16,56},{24,64},{32,72},{40,80},{48,88},{56,96},{64,... | collective-permute-start | bytes 98312 | tf_op jit(solution)/shard_map/ppermute | solution.py:16
  73.2 3.9 %copy-start.17 = (bf16[128,1,128]{2,0,1:T(8,128)(2,1)S(1)}, bf16[128,1,128]{2,0,1:T(8,128)(2,1)}, u32[]{:S(2)}) copy-start(bf16[128,1,128]{2,0,1:T(8,128)(2,1)} %copy-done.16) | copy-start | bytes 98308
  79.4 30.9 %copy-start.7 = (bf16[128,1024]{1,0:T(8,128)(2,1)S(1)}, bf16[128,1024]{1,0:T(8,128)(2,1)}, u32[]{:S(2)}) copy-start(bf16[128,1024]{1,0:T(8,128)(2,1)} %param.55) | copy-start | bytes 786436
  79.5 32.1 %collective-permute-start.19 = (f32[128,1,128]{2,0,1:T(8,128)S(1)}, f32[128,1,128]{2,0,1:T(8,128)S(1)}, u32[]{:S(2)}, u32[]{:S(2)}) collective-permute-start(f32[128,1,128]{2,0,1:T(8,128)S(1)} %get-tuple-element.766), channel_id=1, source_target_pairs={{40,0},{48,8},{56,16},{64,24},{72,32},{80,40},{88,48},{96,56},{104... | collective-permute-start | bytes 196616 | tf_op jit(solution)/shard_map/ppermute | solution.py:16
  84.1 29.4 %collective-permute-start.18 = (f32[128,1,128]{2,0,1:T(8,128)S(1)}, f32[128,1,128]{2,0,1:T(8,128)S(1)}, u32[]{:S(2)}, u32[]{:S(2)}) collective-permute-start(f32[128,1,128]{2,0,1:T(8,128)S(1)} %get-tuple-element.765), channel_id=1, source_target_pairs={{32,0},{40,8},{48,16},{56,24},{64,32},{72,40},{80,48},{88,56},{96,... | collective-permute-start | bytes 196616 | tf_op jit(solution)/shard_map/ppermute | solution.py:16
  100.7 24.8 %collective-permute-start.17 = (f32[128,1,128]{2,0,1:T(8,128)S(1)}, f32[128,1,128]{2,0,1:T(8,128)S(1)}, u32[]{:S(2)}, u32[]{:S(2)}) collective-permute-start(f32[128,1,128]{2,0,1:T(8,128)S(1)} %get-tuple-element.764), channel_id=1, source_target_pairs={{24,0},{32,8},{40,16},{48,24},{56,32},{64,40},{72,48},{80,56},{88,... | collective-permute-start | bytes 196616 | tf_op jit(solution)/shard_map/ppermute | solution.py:16
  105.9 23.6 %collective-permute-start.16 = (f32[128,1,128]{2,0,1:T(8,128)S(1)}, f32[128,1,128]{2,0,1:T(8,128)S(1)}, u32[]{:S(2)}, u32[]{:S(2)}) collective-permute-start(f32[128,1,128]{2,0,1:T(8,128)S(1)} %get-tuple-element.763), channel_id=1, source_target_pairs={{16,0},{24,8},{32,16},{40,24},{48,32},{56,40},{64,48},{72,56},{80,... | collective-permute-start | bytes 196616 | tf_op jit(solution)/shard_map/ppermute | solution.py:16
  107.9 24.8 %collective-permute-start.15 = (f32[128,1,128]{2,0,1:T(8,128)S(1)}, f32[128,1,128]{2,0,1:T(8,128)S(1)}, u32[]{:S(2)}, u32[]{:S(2)}) collective-permute-start(f32[128,1,128]{2,0,1:T(8,128)S(1)} %get-tuple-element.762), channel_id=1, source_target_pairs={{8,0},{16,8},{24,16},{32,24},{40,32},{48,40},{56,48},{64,56},{72,6... | collective-permute-start | bytes 196616 | tf_op jit(solution)/shard_map/ppermute | solution.py:16
  110.8 23.8 %copy-start.9 = (f32[128,1,128]{2,0,1:T(8,128)S(1)}, f32[128,1,128]{2,0,1:T(8,128)}, u32[]{:S(2)}) copy-start(f32[128,1,128]{2,0,1:T(8,128)} %convolution_bitcast_fusion.28) | copy-start | bytes 196612
  111.6 30.9 %collective-permute-start.14 = (f32[128,1,128]{2,0,1:T(8,128)S(1)}, f32[128,1,128]{2,0,1:T(8,128)S(1)}, u32[]{:S(2)}, u32[]{:S(2)}) collective-permute-start(f32[128,1,128]{2,0,1:T(8,128)S(1)} %get-tuple-element.426), channel_id=1, source_target_pairs={{40,0},{48,8},{56,16},{64,24},{72,32},{80,40},{88,48},{96,56},{104... | collective-permute-start | bytes 196616 | tf_op jit(solution)/shard_map/ppermute | solution.py:16
  113.5 28.9 %collective-permute-start.13 = (f32[128,1,128]{2,0,1:T(8,128)S(1)}, f32[128,1,128]{2,0,1:T(8,128)S(1)}, u32[]{:S(2)}, u32[]{:S(2)}) collective-permute-start(f32[128,1,128]{2,0,1:T(8,128)S(1)} %get-tuple-element.425), channel_id=1, source_target_pairs={{32,0},{40,8},{48,16},{56,24},{64,32},{72,40},{80,48},{88,56},{96,... | collective-permute-start | bytes 196616 | tf_op jit(solution)/shard_map/ppermute | solution.py:16
  125.5 17.0 %collective-permute-start.12 = (f32[128,1,128]{2,0,1:T(8,128)S(1)}, f32[128,1,128]{2,0,1:T(8,128)S(1)}, u32[]{:S(2)}, u32[]{:S(2)}) collective-permute-start(f32[128,1,128]{2,0,1:T(8,128)S(1)} %get-tuple-element.424), channel_id=1, source_target_pairs={{24,0},{32,8},{40,16},{48,24},{56,32},{64,40},{72,48},{80,56},{88,... | collective-permute-start | bytes 196616 | tf_op jit(solution)/shard_map/ppermute | solution.py:16
  129.6 12.9 %collective-permute-start.11 = (f32[128,1,128]{2,0,1:T(8,128)S(1)}, f32[128,1,128]{2,0,1:T(8,128)S(1)}, u32[]{:S(2)}, u32[]{:S(2)}) collective-permute-start(f32[128,1,128]{2,0,1:T(8,128)S(1)} %get-tuple-element.423), channel_id=1, source_target_pairs={{16,0},{24,8},{32,16},{40,24},{48,32},{56,40},{64,48},{72,56},{80,... | collective-permute-start | bytes 196616 | tf_op jit(solution)/shard_map/ppermute | solution.py:16
  132.7 9.8 %collective-permute-start.10 = (f32[128,1,128]{2,0,1:T(8,128)S(1)}, f32[128,1,128]{2,0,1:T(8,128)S(1)}, u32[]{:S(2)}, u32[]{:S(2)}) collective-permute-start(f32[128,1,128]{2,0,1:T(8,128)S(1)} %get-tuple-element.422), channel_id=1, source_target_pairs={{8,0},{16,8},{24,16},{32,24},{40,32},{48,40},{56,48},{64,56},{72,6... | collective-permute-start | bytes 196616 | tf_op jit(solution)/shard_map/ppermute | solution.py:16
  135.2 15.2 %all-to-all-start.3 = ((bf16[8,16,128]{2,1,0:T(8,128)(2,1)}), bf16[8,16,128]{2,1,0:T(8,128)(2,1)S(1)}, u32[]{:S(2)}, u32[]{:S(2)}) async-start(bf16[8,16,128]{2,1,0:T(8,128)(2,1)} %bitcast.237), calls=%async_computation.3 | async-start | bytes 65536 | tf_op jit(solution)/shard_map/all_to_all | solution.py:163
  150.5 11.3 %all-to-all-start.2 = ((bf16[8,16,128]{2,1,0:T(8,128)(2,1)}), bf16[8,16,128]{2,1,0:T(8,128)(2,1)S(1)}, u32[]{:S(2)}, u32[]{:S(2)}) async-start(bf16[8,16,128]{2,1,0:T(8,128)(2,1)} %bitcast.231), calls=%async_computation.2 | async-start | bytes 65536 | tf_op jit(solution)/shard_map/all_to_all | solution.py:162
  (14 other events, 18.6 us)
where the time goes:
time: 164 us; the launch traced here: 162 us
  starting transfers between devices  112 us (68%)
  local copies, waits for them, and re-layouts  17.1 us (10%)
  waiting for transfers between devices  14.7 us (9%)
  matrix products  7.11 us (4%)
  other arithmetic  5.84 us (4%)
  between operations  4.76 us (3%)
    ppermute x20, starting transfers between devices, passed_along(): return lax.ppermute(block, axis, route)  87.3 us
    all_to_all x1, waiting for transfers between devices, per_device(): lax.all_to_all(grad_v, 'head', split_axis=0, concat_axis=1, tiled=True)  7.33 us
    all_to_all x1, waiting for transfers between devices, per_device(): lax.all_to_all(grad_k, 'head', split_axis=0, concat_axis=1, tiled=True)  7.33 us
    all_to_all x1, starting transfers between devices, per_device(): lax.all_to_all(keys, 'head', split_axis=1, concat_axis=0, tiled=True)  7.23 us
    all_to_all x1, starting transfers between devices, per_device(): lax.all_to_all(values, 'head', split_axis=1, concat_axis=0, tiled=True)  7.21 us
    all_to_all x1, starting transfers between devices, per_device(): lax.all_to_all(grad_v, 'head', split_axis=0, concat_axis=1, tiled=True)  7.2 us
    unnamed x47, local copies, waits for them, and re-layouts  6.78 us
    another operation x14, local copies, waits for them, and re-layouts  4.59 us
  transfers between devices with their start and end apart: 24, of which 2 were waited for; matrix products, arithmetic and copies ran while one was open for 11% of the time, Pallas kernels for 0%

commit v1 on v0

v1 whole, which is shorter than its diff:
```python
import functools

import jax
import jax.numpy as jnp
from jax import lax
from jax.experimental import pallas as pl
from jax.experimental.pallas import tpu as pltpu
from jax.sharding import PartitionSpec as P

HEAD_SIZE = 128
SCALE = HEAD_SIZE ** (-0.5)
LOG2E = 1.4426950408889634
big_negative = -1e30
MESH = pl.DeviceIdType.MESH
F32 = jnp.float32
BF16 = jnp.bfloat16

OWN = 0
NEAR = 1
FAR = 2
CROSS = 3
NEAR_SIB = 4
FAR_SIB = 5
ROLES = 6


def kernel(
    n_ctx,
    n_head,
    tokens,
    heads,
    q_hbm,
    k_hbm,
    v_hbm,
    g_hbm,
    len_hbm,
    att_hbm,
    dq_hbm,
    dk_out,
    dv_out,
    k_in,
    v_in,
    lens,
    q_rows,
    g_rows,
    q_cols,
    g_cols,
    kv_stage,
    kv,
    k_cols,
    v_cols,
    probs,
    dprobs,
    dscores,
    part,
    back,
    grad_stage,
    grad_in,
    att,
    dq,
    in_sem,
    out_sem,
    y_send,
    y_recv,
    c_send,
    c_recv,
    b_send,
    b_recv,
    z_send,
    z_recv,
):
    d = HEAD_SIZE
    c = lax.axis_index("ctx")
    h = lax.axis_index("head")
    core = lax.rem(c, 2)
    piece = tokens // n_head
    width = heads * tokens

    def ctx_at(distance):
        return lax.rem(c + distance + n_ctx, n_ctx)

    sibling = c + 1 - 2 * core
    cross_to = ctx_at(1 + 4 * core)
    cross_from = ctx_at(4 * core - 5)

    loads = [
        pltpu.make_async_copy(k_hbm, k_in, in_sem.at[0]),
        pltpu.make_async_copy(v_hbm, v_in, in_sem.at[1]),
        pltpu.make_async_copy(len_hbm, lens, in_sem.at[2]),
    ]
    q_loads, g_loads = [], []
    for r in range(heads):
        cols, rows = pl.ds(r * d, d), pl.ds(r * tokens, tokens)
        q_loads.append(
            pltpu.make_async_copy(q_hbm.at[:, cols], q_rows.at[rows, :], in_sem.at[3 + r])
        )
        g_loads.append(
            pltpu.make_async_copy(g_hbm.at[:, cols], g_rows.at[rows, :], in_sem.at[3 + heads + r])
        )
    for load in loads + q_loads + g_loads:
        load.start()

    barrier = pltpu.get_barrier_semaphore()
    peers = [(c, lax.rem(h + step, n_head)) for step in range(1, n_head)]
    peers += [(ctx_at(step), h) for step in (2, -2, 4, -4)]
    peers += [(sibling, h), (jnp.where(core == 0, cross_from, cross_to), h)]
    for peer in peers:
        pl.semaphore_signal(barrier, inc=1, device_id=peer, device_id_type=MESH)

    loads[0].wait()
    loads[1].wait()
    for r in range(n_head):
        cols = slice(r * d, (r + 1) * d)
        kv_stage[r, 0] = k_in[:, cols]
        kv_stage[r, 1] = v_in[:, cols]
    kv[OWN, h] = kv_stage[h]
    pl.semaphore_wait(barrier, len(peers))

    def send(src, dst, send_sem, recv_sem, to):
        copy = pltpu.make_async_remote_copy(
            src_ref=src,
            dst_ref=dst,
            send_sem=send_sem,
            recv_sem=recv_sem,
            device_id=to,
            device_id_type=MESH,
        )
        copy.start()
        return copy

    y_copies = []
    for step in range(1, n_head):
        to = lax.rem(h + step, n_head)
        y_copies.append(
            send(kv_stage.at[to], kv.at[OWN, h], y_send.at[step], y_recv.at[step], (c, to))
        )

    loads[2].wait()
    ids_row = lax.broadcasted_iota(jnp.int32, (128, 128), 0)
    ids_col = lax.broadcasted_iota(jnp.int32, (128, 128), 1)
    ends = jnp.sum(
        jnp.where(ids_col <= ids_row, jnp.broadcast_to(lens[...], (128, 128)), 0).astype(F32),
        axis=1,
        keepdims=True,
    ).astype(jnp.int32)
    place = c * tokens + ids_col
    starts = jnp.max(jnp.where(ends <= place, ends, 0).astype(F32), axis=0, keepdims=True)
    starts = starts.astype(jnp.int32) - c * tokens
    starts = jnp.concatenate([starts] * 2, axis=1)

    for r in range(heads):
        cols, rows = slice(r * d, (r + 1) * d), slice(r * tokens, (r + 1) * tokens)
        q_loads[r].wait()
        q_cols[:, cols] = q_rows[rows, :].T
        g_loads[r].wait()
        g_cols[:, cols] = g_rows[rows, :].T

    for copy in y_copies:
        copy.wait_recv()
    c_copies = [
        send(kv.at[OWN], kv.at[FAR], c_send.at[FAR], c_recv.at[FAR], (ctx_at(4), h)),
        send(kv.at[OWN], kv.at[CROSS], c_send.at[CROSS], c_recv.at[CROSS], (cross_to, h)),
        send(kv.at[OWN], kv.at[NEAR], c_send.at[NEAR], c_recv.at[NEAR], (ctx_at(2), h)),
    ]

    chunk = 2 * tokens
    chunks = width // chunk
    key_ids = lax.broadcasted_iota(jnp.int32, (tokens, chunk), 0)
    query_ids = lax.rem(lax.broadcasted_iota(jnp.int32, (tokens, chunk), 1), tokens)
    back_by = [0, 2, 4, 5 - 4 * core, 1 + 2 * core, 3 + 2 * core]
    tops, totals, deltas = {}, {}, {}

    def forward(role):
        k_block = kv[role, :, 0].reshape(tokens, d)
        v_block = kv[role, :, 1].reshape(tokens, d)
        cols = slice(role * tokens, (role + 1) * tokens)
        k_cols[:, cols] = k_block.T
        v_cols[:, cols] = v_block.T
        visible = key_ids - back_by[role] * tokens >= starts
        if role == OWN:
            visible = visible & (key_ids <= query_ids)
        for j in range(chunks):
            qs = slice(j * chunk, (j + 1) * chunk)
            scores = jnp.dot(k_block, q_cols[:, qs], preferred_element_type=F32)
            scores = jnp.where(visible, scores, big_negative)
            top = jnp.max(scores, axis=0, keepdims=True)
            grown = jnp.exp2((scores - top) * (SCALE * LOG2E))
            dp = jnp.dot(v_block, g_cols[:, qs], preferred_element_type=F32)
            tops[role, j] = top
            totals[role, j] = jnp.sum(grown, axis=0, keepdims=True)
            deltas[role, j] = jnp.sum(grown * dp, axis=0, keepdims=True)
            probs[cols, qs] = grown.astype(BF16)
            dprobs[cols, qs] = dp

    forward(OWN)
    c_copies[2].wait_recv()
    c_copies.append(
        send(kv.at[NEAR], kv.at[NEAR_SIB], c_send.at[NEAR_SIB], c_recv.at[NEAR_SIB], (sibling, h))
    )
    c_copies[0].wait_recv()
    c_copies.append(
        send(kv.at[FAR], kv.at[FAR_SIB], c_send.at[FAR_SIB], c_recv.at[FAR_SIB], (sibling, h))
    )
    forward(NEAR)
    forward(FAR)
    c_copies[1].wait_recv()
    forward(CROSS)
    c_copies[3].wait_recv()
    forward(NEAR_SIB)
    c_copies[4].wait_recv()
    forward(FAR_SIB)

    factors, delta = {}, {}
    for j in range(chunks):
        top = functools.reduce(jnp.maximum, [tops[role, j] for role in range(ROLES)])
        lift = [jnp.exp2((tops[role, j] - top) * (SCALE * LOG2E)) for role in range(ROLES)]
        total = sum(lift[role] * totals[role, j] for role in range(ROLES))
        for role in range(ROLES):
            factors[role, j] = lift[role] / total
        delta[j] = sum(factors[role, j] * deltas[role, j] for role in range(ROLES))

    def backward(role):
        rows = slice(role * tokens, (role + 1) * tokens)
        for j in range(chunks):
            qs = slice(j * chunk, (j + 1) * chunk)
            p = probs[rows, qs].astype(F32) * factors[role, j]
            probs[rows, qs] = p.astype(BF16)
            dscores[rows, qs] = (p * (dprobs[rows, qs] - delta[j])).astype(BF16)
        dk_part = jnp.dot(dscores[rows, :], q_rows[...], preferred_element_type=F32) * SCALE
        dv_part = jnp.dot(probs[rows, :], g_rows[...], preferred_element_type=F32)
        return dk_part, dv_part

    def put(where, dk_part, dv_part):
        where[:, 0] = dk_part.astype(BF16).reshape(n_head, piece, d)
        where[:, 1] = dv_part.astype(BF16).reshape(n_head, piece, d)

    def with_back(slot, dk_part, dv_part):
        dk_part = dk_part + back[slot, :, 0].reshape(tokens, d).astype(F32)
        dv_part = dv_part + back[slot, :, 1].reshape(tokens, d).astype(F32)
        return dk_part, dv_part

    b_copies = {}

    def send_back(role, to):
        b_copies[role] = send(
            part.at[role], back.at[role], b_send.at[role], b_recv.at[role], (to, h)
        )

    put(part.at[FAR_SIB], *backward(FAR_SIB))
    send_back(FAR_SIB, sibling)
    put(part.at[NEAR_SIB], *backward(NEAR_SIB))
    send_back(NEAR_SIB, sibling)
    put(part.at[CROSS], *backward(CROSS))
    send_back(CROSS, cross_from)
    far_grads = backward(FAR)
    b_copies[FAR_SIB].wait_recv()
    put(part.at[FAR], *with_back(FAR_SIB, *far_grads))
    send_back(FAR, ctx_at(-4))
    near_grads = backward(NEAR)
    b_copies[NEAR_SIB].wait_recv()
    put(part.at[NEAR], *with_back(NEAR_SIB, *near_grads))
    send_back(NEAR, ctx_at(-2))
    own_grads = backward(OWN)

    for j in range(chunks):
        qs = slice(j * chunk, (j + 1) * chunk)
        out = jnp.dot(v_cols[...], probs[:, qs], preferred_element_type=F32).astype(BF16)
        grad = jnp.dot(k_cols[...], dscores[:, qs], preferred_element_type=F32) * SCALE
        grad = grad.astype(BF16)
        for i in range(chunk // tokens):
            r = j * (chunk // tokens) + i
            att[:, r * d : (r + 1) * d] = out[:, i * tokens : (i + 1) * tokens].T
            dq[:, r * d : (r + 1) * d] = grad[:, i * tokens : (i + 1) * tokens].T
    stores = [
        pltpu.make_async_copy(att, att_hbm, out_sem.at[0]),
        pltpu.make_async_copy(dq, dq_hbm, out_sem.at[1]),
    ]
    for store in stores:
        store.start()

    for role in (CROSS, NEAR, FAR):
        b_copies[role].wait_recv()
        own_grads = with_back(role, *own_grads)
    put(grad_stage, *own_grads)
    z_copies = []
    for step in range(1, n_head):
        to = lax.rem(h + step, n_head)
        z_copies.append(
            send(grad_stage.at[to], grad_in.at[h], z_send.at[step], z_recv.at[step], (c, to))
        )
    grad_in[h] = grad_stage[h]
    for copy in z_copies:
        copy.wait_recv()
    for r in range(n_head):
        dk_out[:, r * d : (r + 1) * d] = grad_in[r, 0]
        dv_out[:, r * d : (r + 1) * d] = grad_in[r, 1]

    for copy in y_copies + c_copies + list(b_copies.values()) + z_copies:
        copy.wait_send()
    for store in stores:
        store.wait()


def per_device(n_ctx, n_head, queries, keys, values, output_gradient, doc_lengths):
    tokens = queries.shape[0]
    piece = keys.shape[0]
    d = HEAD_SIZE
    heads = queries.shape[1] // d
    width = heads * tokens
    docs = doc_lengths.shape[0]
    any_spec = pl.BlockSpec(memory_space=pl.ANY)
    vmem_spec = pl.BlockSpec(memory_space=pltpu.VMEM)
    block = (n_head, 2, piece, d)
    dma = pltpu.SemaphoreType.DMA
    return pl.pallas_call(
        functools.partial(kernel, n_ctx, n_head, tokens, heads),
        out_shape=(
            jax.ShapeDtypeStruct(queries.shape, BF16),
            jax.ShapeDtypeStruct(queries.shape, BF16),
            jax.ShapeDtypeStruct(keys.shape, BF16),
            jax.ShapeDtypeStruct(values.shape, BF16),
        ),
        in_specs=[any_spec] * 5,
        out_specs=(any_spec, any_spec, vmem_spec, vmem_spec),
        scratch_shapes=[
            pltpu.VMEM(keys.shape, BF16),
            pltpu.VMEM(values.shape, BF16),
            pltpu.VMEM((1, docs), jnp.int32),
            pltpu.VMEM((width, d), BF16),
            pltpu.VMEM((width, d), BF16),
            pltpu.VMEM((d, width), BF16),
            pltpu.VMEM((d, width), BF16),
            pltpu.VMEM(block, BF16),
            pltpu.VMEM((ROLES, *block), BF16),
            pltpu.VMEM((d, ROLES * tokens), BF16),
            pltpu.VMEM((d, ROLES * tokens), BF16),
            pltpu.VMEM((ROLES * tokens, width), BF16),
            pltpu.VMEM((ROLES * tokens, width), F32),
            pltpu.VMEM((ROLES * tokens, width), BF16),
            pltpu.VMEM((ROLES, *block), BF16),
            pltpu.VMEM((ROLES, *block), BF16),
            pltpu.VMEM(block, BF16),
            pltpu.VMEM(block, BF16),
            pltpu.VMEM((tokens, width), BF16),
            pltpu.VMEM((tokens, width), BF16),
            dma((3 + 2 * heads,)),
            dma((2,)),
            dma((n_head,)),
            dma((n_head,)),
            dma((ROLES,)),
            dma((ROLES,)),
            dma((ROLES,)),
            dma((ROLES,)),
            dma((n_head,)),
            dma((n_head,)),
        ],
        compiler_params=pltpu.CompilerParams(
            collective_id=0, has_side_effects=True, vmem_limit_bytes=40 * 1024 * 1024
        ),
    )(queries, keys, values, output_gradient, doc_lengths.reshape(1, docs))


def solution(mesh):
    n_ctx, n_head = mesh.shape["ctx"], mesh.shape["head"]
    return jax.shard_map(
        functools.partial(per_device, n_ctx, n_head),
        mesh=mesh,
        in_specs=(
            P("ctx", "head"),
            P(("ctx", "head"), None),
            P(("ctx", "head"), None),
            P("ctx", "head"),
            P(),
        ),
        out_specs=(
            P("ctx", "head"),
            P("ctx", "head"),
            P(("ctx", "head"), None),
            P(("ctx", "head"), None),
        ),
        check_vma=False,
    )
```

time: 164 us -> 46.3 us (0.28)
  the two profiles are of different devices: /device:TPU:320 before, /device:TPU:1 now
where the time goes in v1:
time: 46.3 us; the launch traced here: 46 us
  Pallas kernels  38.7 us (84%)
  local copies, waits for them, and re-layouts  6.7 us (14%)
  between operations  0.65 us (1%)
    pallas_call x1, Pallas kernels, per_device(): pl.pallas_call(functools.partial(kernel, n_ctx, n_head, tokens, heads), o...  38.7 us
    unnamed x14, local copies, waits for them, and re-layouts  6.7 us

profile of v1, /device:TPU:1, one launch (start us, length us, event | category | flops | bytes accessed | tf_op | source)
XLA Modules:
  0.0 46.0 jit_solution(2943661482513210032)
XLA Ops:
  0.6 0.0 copy-start.4
  0.6 0.6 %copy-done.4 = s32[128]{0:T(128)S(1)} copy-done((s32[128]{0:T(128)S(1)}, s32[128]{0:T(128)}, u32[]{:S(2)}) %copy-start.4) | copy-done | bytes 536
  1.3 0.0 copy-start
  1.3 0.9 %copy-done = bf16[128,1024]{1,0:T(8,128)(2,1)S(1)} copy-done((bf16[128,1024]{1,0:T(8,128)(2,1)S(1)}, bf16[128,1024]{1,0:T(8,128)(2,1)}, u32[]{:S(2)}) %copy-start) | copy-done | bytes 262168
  2.2 0.0 copy-start.1
  2.2 0.9 %copy-done.1 = bf16[128,1024]{1,0:T(8,128)(2,1)S(1)} copy-done((bf16[128,1024]{1,0:T(8,128)(2,1)S(1)}, bf16[128,1024]{1,0:T(8,128)(2,1)}, u32[]{:S(2)}) %copy-start.1) | copy-done | bytes 262168
  3.2 0.0 copy-start.2
  3.2 0.8 %copy-done.2 = bf16[16,1024]{1,0:T(8,128)(2,1)S(1)} copy-done((bf16[16,1024]{1,0:T(8,128)(2,1)S(1)}, bf16[16,1024]{1,0:T(8,128)(2,1)}, u32[]{:S(2)}) %copy-start.2) | copy-done | bytes 32792
  3.9 0.0 copy-start.3
  4.0 0.8 %copy-done.3 = bf16[16,1024]{1,0:T(8,128)(2,1)S(1)} copy-done((bf16[16,1024]{1,0:T(8,128)(2,1)S(1)}, bf16[16,1024]{1,0:T(8,128)(2,1)}, u32[]{:S(2)}) %copy-start.3) | copy-done | bytes 32792
  4.7 38.7 %shard_map.84 = (bf16[128,1024]{1,0:T(8,128)(2,1)S(1)}, bf16[128,1024]{1,0:T(8,128)(2,1)S(1)}, bf16[16,1024]{1,0:T(8,128)(2,1)S(1)}, bf16[16,1024]{1,0:T(8,128)(2,1)S(1)}) custom-call(bf16[128,1024]{1,0:T(8,128)(2,1)S(1)} %copy-done, bf16[16,1024]{1,0:T(8,128)(2,1)S(1)} %copy-done.2, bf16[16,1024]{1,0:T(8,128)(2,1)S(1)} %copy-done.3, ...), custom_call_target="tpu_custom_call" | custom-call | tf_op jit(solution)/shard_map/pallas_call | solution.py:315
  43.4 0.7 %copy.13 = bf16[128,1024]{1,0:T(8,128)(2,1)} copy(bf16[128,1024]{1,0:T(8,128)(2,1)S(1)} %get-tuple-element.8) | data formatting | bytes 524288
  44.1 0.7 %copy.14 = bf16[128,1024]{1,0:T(8,128)(2,1)} copy(bf16[128,1024]{1,0:T(8,128)(2,1)S(1)} %get-tuple-element.9) | data formatting | bytes 524288
  44.8 0.6 %copy.15 = bf16[16,1024]{1,0:T(8,128)(2,1)} copy(bf16[16,1024]{1,0:T(8,128)(2,1)S(1)} %get-tuple-element.10) | data formatting | bytes 65536
  45.4 0.6 %copy.16 = bf16[16,1024]{1,0:T(8,128)(2,1)} copy(bf16[16,1024]{1,0:T(8,128)(2,1)S(1)} %get-tuple-element.11) | data formatting | bytes 65536
Async XLA Ops:
  0.6 0.7 %copy-start.4 = (s32[128]{0:T(128)S(1)}, s32[128]{0:T(128)}, u32[]{:S(2)}) copy-start(s32[128]{0:T(128)} %param.9) | copy-start | bytes 1540
  1.3 0.9 %copy-start = (bf16[128,1024]{1,0:T(8,128)(2,1)S(1)}, bf16[128,1024]{1,0:T(8,128)(2,1)}, u32[]{:S(2)}) copy-start(bf16[128,1024]{1,0:T(8,128)(2,1)} %q_hbm.1) | copy-start | bytes 786436
  2.2 0.9 %copy-start.1 = (bf16[128,1024]{1,0:T(8,128)(2,1)S(1)}, bf16[128,1024]{1,0:T(8,128)(2,1)}, u32[]{:S(2)}) copy-start(bf16[128,1024]{1,0:T(8,128)(2,1)} %g_hbm.1) | copy-start | bytes 786436
  3.2 0.8 %copy-start.2 = (bf16[16,1024]{1,0:T(8,128)(2,1)S(1)}, bf16[16,1024]{1,0:T(8,128)(2,1)}, u32[]{:S(2)}) copy-start(bf16[16,1024]{1,0:T(8,128)(2,1)} %k_hbm.1) | copy-start | bytes 98308
  3.9 0.8 %copy-start.3 = (bf16[16,1024]{1,0:T(8,128)(2,1)S(1)}, bf16[16,1024]{1,0:T(8,128)(2,1)}, u32[]{:S(2)}) copy-start(bf16[16,1024]{1,0:T(8,128)(2,1)} %v_hbm.1) | copy-start | bytes 98308

commit v2 on v1

--- a/solution.py
+++ b/solution.py
@@ -22,6 +22,38 @@
 NEAR_SIB = 4
 FAR_SIB = 5
 ROLES = 6
+
+
+class Message:
+    def __init__(self, src, dst, send_sem, recv_sem, to, sends=None, receives=None):
+        self.copy = pltpu.make_async_remote_copy(
+            src_ref=src,
+            dst_ref=dst,
+            send_sem=send_sem,
+            recv_sem=recv_sem,
+            device_id=to,
+            device_id_type=MESH,
+        )
+        self.sends, self.receives = sends, receives
+
+    def start(self):
+        run_if(self.sends, self.copy.start)
+
+    def wait_recv(self):
+        run_if(self.receives, self.copy.wait_recv)
+
+    def wait_send(self):
+        run_if(self.sends, self.copy.wait_send)
+
+
+def run_if(condition, action):
+    if condition is None:
+        action()
+        return
+
+    @pl.when(condition)
+    def _():
+        action()
 
 
 def kernel(
@@ -34,8 +66,8 @@
     v_hbm,
     g_hbm,
     len_hbm,
-    att_hbm,
-    dq_hbm,
+    att,
+    dq,
     dk_out,
     dv_out,
     k_in,
@@ -56,10 +88,7 @@
     back,
     grad_stage,
     grad_in,
-    att,
-    dq,
     in_sem,
-    out_sem,
     y_send,
     y_recv,
     c_send,
@@ -76,12 +105,11 @@
     piece = tokens // n_head
     width = heads * tokens
 
-    def ctx_at(distance):
-        return lax.rem(c + distance + n_ctx, n_ctx)
-
     sibling = c + 1 - 2 * core
-    cross_to = ctx_at(1 + 4 * core)
-    cross_from = ctx_at(4 * core - 5)
+    cross_to = c + 1 + 4 * core
+    cross_from = c + 4 * core - 5
+    has_from = {NEAR: c >= 2, FAR: c >= 4, CROSS: cross_from >= 0}
+    has_to = {NEAR: c + 2 < n_ctx, FAR: c + 4 < n_ctx, CROSS: cross_to < n_ctx}
 
     loads = [
         pltpu.make_async_copy(k_hbm, k_in, in_sem.at[0]),
@@ -100,12 +128,39 @@
     for load in loads + q_loads + g_loads:
         load.start()
 
+    for role in (NEAR, FAR, CROSS):
+
+        @pl.when(jnp.logical_not(has_from[role]))
+        def _(role=role):
+            kv[role] = jnp.zeros(kv.shape[1:], BF16)
+
+        @pl.when(jnp.logical_not(has_to[role]))
+        def _(role=role):
+            back[role] = jnp.zeros(back.shape[1:], BF16)
+
     barrier = pltpu.get_barrier_semaphore()
-    peers = [(c, lax.rem(h + step, n_head)) for step in range(1, n_head)]
-    peers += [(ctx_at(step), h) for step in (2, -2, 4, -4)]
-    peers += [(sibling, h), (jnp.where(core == 0, cross_from, cross_to), h)]
-    for peer in peers:
+
+    def greet(peer):
         pl.semaphore_signal(barrier, inc=1, device_id=peer, device_id_type=MESH)
+
+    for step in range(1, n_head):
+        greet((c, lax.rem(h + step, n_head)))
+    greet((sibling, h))
+    n_peers = n_head
+    far_cross = jnp.where(core == 0, cross_from, cross_to)
+    for there, peer in (
+        (has_from[NEAR], c - 2),
+        (has_to[NEAR], c + 2),
+        (has_from[FAR], c - 4),
+        (has_to[FAR], c + 4),
+        ((far_cross >= 0) & (far_cross < n_ctx), far_cross),
+    ):
+
+        @pl.when(there)
+        def _(peer=peer):
+            greet((peer, h))
+
+        n_peers = n_peers + jnp.where(there, 1, 0)
 
     loads[0].wait()
     loads[1].wait()
@@ -114,17 +169,10 @@
         kv_stage[r, 0] = k_in[:, cols]
         kv_stage[r, 1] = v_in[:, cols]
     kv[OWN, h] = kv_stage[h]
-    pl.semaphore_wait(barrier, len(peers))
-
-    def send(src, dst, send_sem, recv_sem, to):
-        copy = pltpu.make_async_remote_copy(
-            src_ref=src,
-            dst_ref=dst,
-            send_sem=send_sem,
-            recv_sem=recv_sem,
-            device_id=to,
-            device_id_type=MESH,
-        )
+    pl.semaphore_wait(barrier, n_peers)
+
+    def send(src, dst, send_sem, recv_sem, to, sends=None, receives=None):
+        copy = Message(src, dst, send_sem, recv_sem, to, sends, receives)
         copy.start()
         return copy
 
@@ -158,9 +206,11 @@
     for copy in y_copies:
         copy.wait_recv()
     c_copies = [
-        send(kv.at[OWN], kv.at[FAR], c_send.at[FAR], c_recv.at[FAR], (ctx_at(4), h)),
-        send(kv.at[OWN], kv.at[CROSS], c_send.at[CROSS], c_recv.at[CROSS], (cross_to, h)),
-        send(kv.at[OWN], kv.at[NEAR], c_send.at[NEAR], c_recv.at[NEAR], (ctx_at(2), h)),
+        send(
+            kv.at[OWN], kv.at[role], c_send.at[role], c_recv.at[role], (to, h),
+            has_to[role], has_from[role],
+        )
+        for role, to in ((FAR, c + 4), (CROSS, cross_to), (NEAR, c + 2))
     ]
 
     chunk = 2 * tokens
@@ -243,7 +293,8 @@
 
     def send_back(role, to):
         b_copies[role] = send(
-            part.at[role], back.at[role], b_send.at[role], b_recv.at[role], (to, h)
+            part.at[role], back.at[role], b_send.at[role], b_recv.at[role], (to, h),
+            has_from.get(role), has_to.get(role),
         )
 
     put(part.at[FAR_SIB], *backward(FAR_SIB))
@@ -255,11 +306,11 @@
     far_grads = backward(FAR)
     b_copies[FAR_SIB].wait_recv()
     put(part.at[FAR], *with_back(FAR_SIB, *far_grads))
-    send_back(FAR, ctx_at(-4))
+    send_back(FAR, c - 4)
     near_grads = backward(NEAR)
     b_copies[NEAR_SIB].wait_recv()
     put(part.at[NEAR], *with_back(NEAR_SIB, *near_grads))
-    send_back(NEAR, ctx_at(-2))
+    send_back(NEAR, c - 2)
     own_grads = backward(OWN)
 
     for j in range(chunks):
@@ -271,13 +322,6 @@
             r = j * (chunk // tokens) + i
             att[:, r * d : (r + 1) * d] = out[:, i * tokens : (i + 1) * tokens].T
             dq[:, r * d : (r + 1) * d] = grad[:, i * tokens : (i + 1) * tokens].T
-    stores = [
-        pltpu.make_async_copy(att, att_hbm, out_sem.at[0]),
-        pltpu.make_async_copy(dq, dq_hbm, out_sem.at[1]),
-    ]
-    for store in stores:
-        store.start()
-
     for role in (CROSS, NEAR, FAR):
         b_copies[role].wait_recv()
         own_grads = with_back(role, *own_grads)
@@ -297,8 +341,6 @@
 
     for copy in y_copies + c_copies + list(b_copies.values()) + z_copies:
         copy.wait_send()
-    for store in stores:
-        store.wait()
 
 
 def per_device(n_ctx, n_head, queries, keys, values, output_gradient, doc_lengths):
@@ -308,7 +350,7 @@
     heads = queries.shape[1] // d
     width = heads * tokens
     docs = doc_lengths.shape[0]
-    any_spec = pl.BlockSpec(memory_space=pl.ANY)
+    hbm_spec = pl.BlockSpec(memory_space=pltpu.HBM)
     vmem_spec = pl.BlockSpec(memory_space=pltpu.VMEM)
     block = (n_head, 2, piece, d)
     dma = pltpu.SemaphoreType.DMA
@@ -320,8 +362,8 @@
             jax.ShapeDtypeStruct(keys.shape, BF16),
             jax.ShapeDtypeStruct(values.shape, BF16),
         ),
-        in_specs=[any_spec] * 5,
-        out_specs=(any_spec, any_spec, vmem_spec, vmem_spec),
+        in_specs=[hbm_spec] * 5,
+        out_specs=(vmem_spec,) * 4,
         scratch_shapes=[
             pltpu.VMEM(keys.shape, BF16),
             pltpu.VMEM(values.shape, BF16),
@@ -341,10 +383,7 @@
             pltpu.VMEM((ROLES, *block), BF16),
             pltpu.VMEM(block, BF16),
             pltpu.VMEM(block, BF16),
-            pltpu.VMEM((tokens, width), BF16),
-            pltpu.VMEM((tokens, width), BF16),
             dma((3 + 2 * heads,)),
-            dma((2,)),
             dma((n_head,)),
             dma((n_head,)),
             dma((ROLES,)),
@@ -357,7 +396,10 @@
         compiler_params=pltpu.CompilerParams(
             collective_id=0, has_side_effects=True, vmem_limit_bytes=40 * 1024 * 1024
         ),
-    )(queries, keys, values, output_gradient, doc_lengths.reshape(1, docs))
+    )(*(
+        pltpu.with_memory_space_constraint(x, pltpu.HBM)
+        for x in (queries, keys, values, output_gradient, doc_lengths.reshape(1, docs))
+    ))
 
 
 def solution(mesh):

time: 46.3 us -> 37 us (0.80)
  the two profiles are of different devices: /device:TPU:1 before, /device:TPU:198 now
where the time goes in v2:
time: 37 us; the launch traced here: 36.8 us
  Pallas kernels  33.5 us (91%)
  local copies, waits for them, and re-layouts  2.64 us (7%)
  between operations  0.64 us (2%)
    pallas_call x1, Pallas kernels, per_device(): pl.pallas_call(functools.partial(kernel, n_ctx, n_head, tokens, heads), o...  33.5 us
    unnamed x4, local copies, waits for them, and re-layouts  2.64 us

profile of v2, /device:TPU:198, one launch (start us, length us, event | category | flops | bytes accessed | tf_op | source)
XLA Modules:
  0.0 36.8 jit_solution(3890421446109983050)
XLA Ops:
  0.6 33.5 %shard_map.84 = (bf16[128,1024]{1,0:T(8,128)(2,1)S(1)}, bf16[128,1024]{1,0:T(8,128)(2,1)S(1)}, bf16[16,1024]{1,0:T(8,128)(2,1)S(1)}, bf16[16,1024]{1,0:T(8,128)(2,1)S(1)}) custom-call(bf16[128,1024]{1,0:T(8,128)(2,1)} %q_hbm.1, bf16[16,1024]{1,0:T(8,128)(2,1)} %k_hbm.1, bf16[16,1024]{1,0:T(8,128)(2,1)} %v_hbm.1, bf16[128,1024]{1,0:T(8,128)(2,1)} %g_hbm.1, ...), custom_call_target="tpu_custom_call" | custom-call | tf_op jit(solution)/shard_map/pallas_call | solution.py:357
  34.2 0.7 %copy.13 = bf16[128,1024]{1,0:T(8,128)(2,1)} copy(bf16[128,1024]{1,0:T(8,128)(2,1)S(1)} %get-tuple-element.8) | data formatting | bytes 524288
  34.9 0.7 %copy.14 = bf16[128,1024]{1,0:T(8,128)(2,1)} copy(bf16[128,1024]{1,0:T(8,128)(2,1)S(1)} %get-tuple-element.9) | data formatting | bytes 524288
  35.6 0.6 %copy.15 = bf16[16,1024]{1,0:T(8,128)(2,1)} copy(bf16[16,1024]{1,0:T(8,128)(2,1)S(1)} %get-tuple-element.10) | data formatting | bytes 65536
  36.2 0.6 %copy.16 = bf16[16,1024]{1,0:T(8,128)(2,1)} copy(bf16[16,1024]{1,0:T(8,128)(2,1)S(1)} %get-tuple-element.11) | data formatting | bytes 65536

commit v3 on v2

--- a/solution.py
+++ b/solution.py
@@ -22,6 +22,10 @@
 NEAR_SIB = 4
 FAR_SIB = 5
 ROLES = 6
+
+
+def ring_steps(n):
+    return sorted(range(n), key=lambda step: (min(step, n - step), step))
 
 
 class Message:
@@ -73,8 +77,8 @@
     k_in,
     v_in,
     lens,
-    q_rows,
-    g_rows,
+    q_in,
+    g_in,
     q_cols,
     g_cols,
     kv_stage,
@@ -104,6 +108,12 @@
     core = lax.rem(c, 2)
     piece = tokens // n_head
     width = heads * tokens
+    steps = ring_steps(n_head)
+    near_slots = n_head // 2 + 1
+    groups = (pl.ds(0, near_slots * 2 * piece), pl.ds(near_slots * 2 * piece, (n_head - near_slots) * 2 * piece))
+
+    def slot_rows(slot):
+        return pl.ds(slot * 2 * piece, 2 * piece)
 
     sibling = c + 1 - 2 * core
     cross_to = c + 1 + 4 * core
@@ -112,31 +122,13 @@
     has_to = {NEAR: c + 2 < n_ctx, FAR: c + 4 < n_ctx, CROSS: cross_to < n_ctx}
 
     loads = [
-        pltpu.make_async_copy(k_hbm, k_in, in_sem.at[0]),
-        pltpu.make_async_copy(v_hbm, v_in, in_sem.at[1]),
-        pltpu.make_async_copy(len_hbm, lens, in_sem.at[2]),
+        pltpu.make_async_copy(source, target, in_sem.at[i])
+        for i, (source, target) in enumerate(
+            ((k_hbm, k_in), (v_hbm, v_in), (len_hbm, lens), (q_hbm, q_in), (g_hbm, g_in))
+        )
     ]
-    q_loads, g_loads = [], []
-    for r in range(heads):
-        cols, rows = pl.ds(r * d, d), pl.ds(r * tokens, tokens)
-        q_loads.append(
-            pltpu.make_async_copy(q_hbm.at[:, cols], q_rows.at[rows, :], in_sem.at[3 + r])
-        )
-        g_loads.append(
-            pltpu.make_async_copy(g_hbm.at[:, cols], g_rows.at[rows, :], in_sem.at[3 + heads + r])
-        )
-    for load in loads + q_loads + g_loads:
-        load.start()
-
-    for role in (NEAR, FAR, CROSS):
-
-        @pl.when(jnp.logical_not(has_from[role]))
-        def _(role=role):
-            kv[role] = jnp.zeros(kv.shape[1:], BF16)
-
-        @pl.when(jnp.logical_not(has_to[role]))
-        def _(role=role):
-            back[role] = jnp.zeros(back.shape[1:], BF16)
+    loads[0].start()
+    loads[1].start()
 
     barrier = pltpu.get_barrier_semaphore()
 
@@ -162,13 +154,15 @@
 
         n_peers = n_peers + jnp.where(there, 1, 0)
 
+    for load in loads[2:]:
+        load.start()
     loads[0].wait()
     loads[1].wait()
     for r in range(n_head):
         cols = slice(r * d, (r + 1) * d)
-        kv_stage[r, 0] = k_in[:, cols]
-        kv_stage[r, 1] = v_in[:, cols]
-    kv[OWN, h] = kv_stage[h]
+        kv_stage[r, :piece] = k_in[:, cols]
+        kv_stage[r, piece:] = v_in[:, cols]
+    kv[OWN, slot_rows(0)] = kv_stage[h]
     pl.semaphore_wait(barrier, n_peers)
 
     def send(src, dst, send_sem, recv_sem, to, sends=None, receives=None):
@@ -176,12 +170,22 @@
         copy.start()
         return copy
 
-    y_copies = []
-    for step in range(1, n_head):
-        to = lax.rem(h + step, n_head)
-        y_copies.append(
-            send(kv_stage.at[to], kv.at[OWN, h], y_send.at[step], y_recv.at[step], (c, to))
+    y_copies = {}
+    for step in reversed(steps[1:]):
+        to, slot = lax.rem(h + step, n_head), steps.index(n_head - step)
+        y_copies[slot] = send(
+            kv_stage.at[to], kv.at[OWN, slot_rows(slot)], y_send.at[slot], y_recv.at[slot], (c, to)
         )
+
+    for role in (NEAR, FAR, CROSS):
+
+        @pl.when(jnp.logical_not(has_from[role]))
+        def _(role=role):
+            kv[role] = jnp.zeros(kv.shape[1:], BF16)
+
+        @pl.when(jnp.logical_not(has_to[role]))
+        def _(role=role):
+            back[role] = jnp.zeros(back.shape[1:], BF16)
 
     loads[2].wait()
     ids_row = lax.broadcasted_iota(jnp.int32, (128, 128), 0)
@@ -196,33 +200,49 @@
     starts = starts.astype(jnp.int32) - c * tokens
     starts = jnp.concatenate([starts] * 2, axis=1)
 
+    c_copies = {}
+
+    def send_on(source, role, to, group):
+        rows = groups[group]
+        c_copies[role, group] = send(
+            kv.at[source, rows],
+            kv.at[role, rows],
+            c_send.at[role, group],
+            c_recv.at[role, group],
+            (to, h),
+            has_to.get(role),
+            has_from.get(role),
+        )
+
+    for group, slots in enumerate((range(1, near_slots), range(near_slots, n_head))):
+        for slot in slots:
+            y_copies[slot].wait_recv()
+        for role, to in ((FAR, c + 4), (CROSS, cross_to), (NEAR, c + 2)):
+            send_on(OWN, role, to, group)
+
+    loads[3].wait()
+    loads[4].wait()
     for r in range(heads):
-        cols, rows = slice(r * d, (r + 1) * d), slice(r * tokens, (r + 1) * tokens)
-        q_loads[r].wait()
-        q_cols[:, cols] = q_rows[rows, :].T
-        g_loads[r].wait()
-        g_cols[:, cols] = g_rows[rows, :].T
-
-    for copy in y_copies:
-        copy.wait_recv()
-    c_copies = [
-        send(
-            kv.at[OWN], kv.at[role], c_send.at[role], c_recv.at[role], (to, h),
-            has_to[role], has_from[role],
-        )
-        for role, to in ((FAR, c + 4), (CROSS, cross_to), (NEAR, c + 2))
-    ]
+        cols = slice(r * d, (r + 1) * d)
+        q_cols[:, cols] = q_in[:, cols].T
+        g_cols[:, cols] = g_in[:, cols].T
 
     chunk = 2 * tokens
     chunks = width // chunk
-    key_ids = lax.broadcasted_iota(jnp.int32, (tokens, chunk), 0)
+    key_rows = lax.broadcasted_iota(jnp.int32, (tokens, chunk), 0)
+    key_slots = key_rows // piece
+    key_steps = jnp.where(key_slots % 2 == 1, (key_slots + 1) // 2, n_head - key_slots // 2)
+    key_ids = lax.rem(h + key_steps, n_head) * piece + lax.rem(key_rows, piece)
     query_ids = lax.rem(lax.broadcasted_iota(jnp.int32, (tokens, chunk), 1), tokens)
     back_by = [0, 2, 4, 5 - 4 * core, 1 + 2 * core, 3 + 2 * core]
     tops, totals, deltas = {}, {}, {}
 
+    def apart(both):
+        both = both.reshape(n_head, 2, piece, d)
+        return both[:, 0].reshape(tokens, d), both[:, 1].reshape(tokens, d)
+
     def forward(role):
-        k_block = kv[role, :, 0].reshape(tokens, d)
-        v_block = kv[role, :, 1].reshape(tokens, d)
+        k_block, v_block = apart(kv[role])
         cols = slice(role * tokens, (role + 1) * tokens)
         k_cols[:, cols] = k_block.T
         v_cols[:, cols] = v_block.T
@@ -243,22 +263,16 @@
             dprobs[cols, qs] = dp
 
     forward(OWN)
-    c_copies[2].wait_recv()
-    c_copies.append(
-        send(kv.at[NEAR], kv.at[NEAR_SIB], c_send.at[NEAR_SIB], c_recv.at[NEAR_SIB], (sibling, h))
-    )
-    c_copies[0].wait_recv()
-    c_copies.append(
-        send(kv.at[FAR], kv.at[FAR_SIB], c_send.at[FAR_SIB], c_recv.at[FAR_SIB], (sibling, h))
-    )
+    for group in range(2):
+        for role, there in ((NEAR, NEAR_SIB), (FAR, FAR_SIB)):
+            c_copies[role, group].wait_recv()
+            send_on(role, there, sibling, group)
     forward(NEAR)
     forward(FAR)
-    c_copies[1].wait_recv()
-    forward(CROSS)
-    c_copies[3].wait_recv()
-    forward(NEAR_SIB)
-    c_copies[4].wait_recv()
-    forward(FAR_SIB)
+    for role in (CROSS, NEAR_SIB, FAR_SIB):
+        for group in range(2):
+            c_copies[role, group].wait_recv()
+        forward(role)
 
     factors, delta = {}, {}
     for j in range(chunks):
@@ -271,31 +285,52 @@
 
     def backward(role):
         rows = slice(role * tokens, (role + 1) * tokens)
+        dk_part = dv_part = 0.0
         for j in range(chunks):
             qs = slice(j * chunk, (j + 1) * chunk)
             p = probs[rows, qs].astype(F32) * factors[role, j]
-            probs[rows, qs] = p.astype(BF16)
-            dscores[rows, qs] = (p * (dprobs[rows, qs] - delta[j])).astype(BF16)
-        dk_part = jnp.dot(dscores[rows, :], q_rows[...], preferred_element_type=F32) * SCALE
-        dv_part = jnp.dot(probs[rows, :], g_rows[...], preferred_element_type=F32)
-        return dk_part, dv_part
+            ds = (p * (dprobs[rows, qs] - delta[j])).astype(BF16)
+            p = p.astype(BF16)
+            probs[rows, qs] = p
+            dscores[rows, qs] = ds
+            dk_part += jnp.dot(ds, by_rows(q_in, j), preferred_element_type=F32)
+            dv_part += jnp.dot(p, by_rows(g_in, j), preferred_element_type=F32)
+        return dk_part * SCALE, dv_part
+
+    def by_rows(ref, j):
+        pair = [
+            ref[:, r * d : (r + 1) * d]
+            for r in range(j * chunk // tokens, (j + 1) * chunk // tokens)
+        ]
+        return jnp.concatenate(pair, axis=0)
+
+    def together(dk_part, dv_part, dtype):
+        pieces = [x.astype(dtype).reshape(n_head, 1, piece, d) for x in (dk_part, dv_part)]
+        return jnp.concatenate(pieces, axis=1).reshape(2 * tokens, d)
 
     def put(where, dk_part, dv_part):
-        where[:, 0] = dk_part.astype(BF16).reshape(n_head, piece, d)
-        where[:, 1] = dv_part.astype(BF16).reshape(n_head, piece, d)
-
-    def with_back(slot, dk_part, dv_part):
-        dk_part = dk_part + back[slot, :, 0].reshape(tokens, d).astype(F32)
-        dv_part = dv_part + back[slot, :, 1].reshape(tokens, d).astype(F32)
-        return dk_part, dv_part
+        where[...] = together(dk_part, dv_part, BF16)
+
+    def with_back(role, dk_part, dv_part):
+        for group in range(2):
+            b_copies[role, group].wait_recv()
+        dk_back, dv_back = apart(back[role])
+        return dk_part + dk_back.astype(F32), dv_part + dv_back.astype(F32)
 
     b_copies = {}
 
     def send_back(role, to):
-        b_copies[role] = send(
-            part.at[role], back.at[role], b_send.at[role], b_recv.at[role], (to, h),
-            has_from.get(role), has_to.get(role),
-        )
+        for group in (1, 0):
+            rows = groups[group]
+            b_copies[role, group] = send(
+                part.at[role, rows],
+                back.at[role, rows],
+                b_send.at[role, group],
+                b_recv.at[role, group],
+                (to, h),
+                has_from.get(role),
+                has_to.get(role),
+            )
 
     put(part.at[FAR_SIB], *backward(FAR_SIB))
     send_back(FAR_SIB, sibling)
@@ -304,11 +339,9 @@
     put(part.at[CROSS], *backward(CROSS))
     send_back(CROSS, cross_from)
     far_grads = backward(FAR)
-    b_copies[FAR_SIB].wait_recv()
     put(part.at[FAR], *with_back(FAR_SIB, *far_grads))
     send_back(FAR, c - 4)
     near_grads = backward(NEAR)
-    b_copies[NEAR_SIB].wait_recv()
     put(part.at[NEAR], *with_back(NEAR_SIB, *near_grads))
     send_back(NEAR, c - 2)
     own_grads = backward(OWN)
@@ -322,25 +355,44 @@
             r = j * (chunk // tokens) + i
             att[:, r * d : (r + 1) * d] = out[:, i * tokens : (i + 1) * tokens].T
             dq[:, r * d : (r + 1) * d] = grad[:, i * tokens : (i + 1) * tokens].T
-    for role in (CROSS, NEAR, FAR):
-        b_copies[role].wait_recv()
-        own_grads = with_back(role, *own_grads)
-    put(grad_stage, *own_grads)
-    z_copies = []
-    for step in range(1, n_head):
-        to = lax.rem(h + step, n_head)
-        z_copies.append(
-            send(grad_stage.at[to], grad_in.at[h], z_send.at[step], z_recv.at[step], (c, to))
-        )
-    grad_in[h] = grad_stage[h]
-    for copy in z_copies:
+    for copy in list(y_copies.values()) + list(c_copies.values()):
+        copy.wait_send()
+    own_sum = together(*own_grads, F32)
+    z_copies = {}
+    for group, slots in ((1, range(near_slots, n_head)), (0, range(near_slots))):
+        rows = slice(groups[group].start, groups[group].start + groups[group].size)
+        for role in (CROSS, FAR, NEAR):
+            b_copies[role, group].wait_recv()
+        total = own_sum[rows]
+        for role in (CROSS, FAR, NEAR):
+            total += back[role, rows].astype(F32)
+        grad_stage[rows] = total.astype(BF16)
+        for slot in reversed(slots):
+            if slot:
+                to = lax.rem(h + steps[slot], n_head)
+                z_copies[slot] = send(
+                    grad_stage.at[slot_rows(slot)],
+                    grad_in.at[h],
+                    z_send.at[slot],
+                    z_recv.at[slot],
+                    (c, to),
+                )
+    grad_in[h] = grad_stage[slot_rows(0)]
+    for copy in b_copies.values():
+        copy.wait_send()
+    for copy in z_copies.values():
         copy.wait_recv()
     for r in range(n_head):
-        dk_out[:, r * d : (r + 1) * d] = grad_in[r, 0]
-        dv_out[:, r * d : (r + 1) * d] = grad_in[r, 1]
-
-    for copy in y_copies + c_copies + list(b_copies.values()) + z_copies:
+        dk_out[:, r * d : (r + 1) * d] = grad_in[r, :piece]
+        dv_out[:, r * d : (r + 1) * d] = grad_in[r, piece:]
+
+    for copy in z_copies.values():
         copy.wait_send()
+
+
+def write_out(*refs):
+    for i in range(4):
+        refs[4 + i][...] = refs[i][...]
 
 
 def per_device(n_ctx, n_head, queries, keys, values, output_gradient, doc_lengths):
@@ -352,9 +404,9 @@
     docs = doc_lengths.shape[0]
     hbm_spec = pl.BlockSpec(memory_space=pltpu.HBM)
     vmem_spec = pl.BlockSpec(memory_space=pltpu.VMEM)
-    block = (n_head, 2, piece, d)
+    block = (2 * tokens, d)
     dma = pltpu.SemaphoreType.DMA
-    return pl.pallas_call(
+    results = pl.pallas_call(
         functools.partial(kernel, n_ctx, n_head, tokens, heads),
         out_shape=(
             jax.ShapeDtypeStruct(queries.shape, BF16),
@@ -368,11 +420,11 @@
             pltpu.VMEM(keys.shape, BF16),
             pltpu.VMEM(values.shape, BF16),
             pltpu.VMEM((1, docs), jnp.int32),
-            pltpu.VMEM((width, d), BF16),
-            pltpu.VMEM((width, d), BF16),
+            pltpu.VMEM((tokens, width), BF16),
+            pltpu.VMEM((tokens, width), BF16),
             pltpu.VMEM((d, width), BF16),
             pltpu.VMEM((d, width), BF16),
-            pltpu.VMEM(block, BF16),
+            pltpu.VMEM((n_head, 2 * piece, d), BF16),
             pltpu.VMEM((ROLES, *block), BF16),
             pltpu.VMEM((d, ROLES * tokens), BF16),
             pltpu.VMEM((d, ROLES * tokens), BF16),
@@ -382,14 +434,14 @@
             pltpu.VMEM((ROLES, *block), BF16),
             pltpu.VMEM((ROLES, *block), BF16),
             pltpu.VMEM(block, BF16),
-            pltpu.VMEM(block, BF16),
-            dma((3 + 2 * heads,)),
+            pltpu.VMEM((n_head, 2 * piece, d), BF16),
+            dma((5,)),
             dma((n_head,)),
             dma((n_head,)),
-            dma((ROLES,)),
-            dma((ROLES,)),
-            dma((ROLES,)),
-            dma((ROLES,)),
+            dma((ROLES, 2)),
+            dma((ROLES, 2)),
+            dma((ROLES, 2)),
+            dma((ROLES, 2)),
             dma((n_head,)),
             dma((n_head,)),
         ],
@@ -400,6 +452,14 @@
         pltpu.with_memory_space_constraint(x, pltpu.HBM)
         for x in (queries, keys, values, output_gradient, doc_lengths.reshape(1, docs))
     ))
+    return pl.pallas_call(
+        write_out,
+        out_shape=tuple(jax.ShapeDtypeStruct(x.shape, x.dtype) for x in results),
+        in_specs=[vmem_spec] * 4,
+        out_specs=(vmem_spec,) * 4,
+        scratch_shapes=[dma((4,))],
+        compiler_params=pltpu.CompilerParams(vmem_limit_bytes=8 * 1024 * 1024),
+    )(*results)
 
 
 def solution(mesh):

time: 37 us -> 34.2 us (0.924)
  local copies, waits for them, and re-layouts: 2.64 us -> 0 us
    unnamed x4 -> x0, local copies, waits for them, and re-layouts: 2.64 us -> none
    pallas_call x1, Pallas kernels: 33.5 us -> 32.6 us  [per_device(): pl.pallas_call(functools.partial(kernel, n_ctx, n_head, tokens, heads), o...]
    pallas_call x0 -> x1, Pallas kernels: none -> 0.87 us  [per_device(): pl.pallas_call(write_out, out_shape=tuple((jax.ShapeDtypeStruct(x.shape,...]
where the time goes in v3:
time: 34.2 us; the launch traced here: 34.1 us
  Pallas kernels  33.4 us (98%)
  between operations  0.64 us (2%)
    pallas_call x1, Pallas kernels, per_device(): pl.pallas_call(functools.partial(kernel, n_ctx, n_head, tokens, heads), o...  32.6 us
    pallas_call x1, Pallas kernels, per_device(): pl.pallas_call(write_out, out_shape=tuple((jax.ShapeDtypeStruct(x.shape,...  0.87 us

profile of v3, /device:TPU:198, one launch (start us, length us, event | category | flops | bytes accessed | tf_op | source)
XLA Modules:
  0.0 34.1 jit_solution(6659728243644731204)
XLA Ops:
  0.6 32.6 %shard_map.84 = (bf16[128,1024]{1,0:T(8,128)(2,1)S(1)}, bf16[128,1024]{1,0:T(8,128)(2,1)S(1)}, bf16[16,1024]{1,0:T(8,128)(2,1)S(1)}, bf16[16,1024]{1,0:T(8,128)(2,1)S(1)}) custom-call(bf16[128,1024]{1,0:T(8,128)(2,1)} %q_hbm.1, bf16[16,1024]{1,0:T(8,128)(2,1)} %k_hbm.1, bf16[16,1024]{1,0:T(8,128)(2,1)} %v_hbm.1, bf16[128,1024]{1,0:T(8,128)(2,1)} %g_hbm.1, ...), custom_call_target="tpu_custom_call" | custom-call | tf_op jit(solution)/shard_map/pallas_call | solution.py:409
  33.2 0.9 %shard_map.85 = (bf16[128,1024]{1,0:T(8,128)(2,1)}, bf16[128,1024]{1,0:T(8,128)(2,1)}, bf16[16,1024]{1,0:T(8,128)(2,1)}, bf16[16,1024]{1,0:T(8,128)(2,1)}) custom-call(bf16[128,1024]{1,0:T(8,128)(2,1)S(1)} %get-tuple-element.8.refs_0_, bf16[128,1024]{1,0:T(8,128)(2,1)S(1)} %get-tuple-element.9.refs_1_, bf16[16,1024]{1,0:T(8,128)(2,1)S(1)} %get-tuple-element.10.refs_2_, ...), custom_call_target="tpu_custom_call" | custom-call | tf_op jit(solution)/shard_map/pallas_call | solution.py:455

commit v4 on v3

--- a/solution.py
+++ b/solution.py
@@ -101,6 +101,7 @@
     b_recv,
     z_send,
     z_recv,
+    ready,
 ):
     d = HEAD_SIZE
     c = lax.axis_index("ctx")
@@ -127,33 +128,27 @@
             ((k_hbm, k_in), (v_hbm, v_in), (len_hbm, lens), (q_hbm, q_in), (g_hbm, g_in))
         )
     ]
+    barrier = pltpu.get_barrier_semaphore()
+
+    def greet(peer):
+        pl.semaphore_signal(barrier, inc=1, device_id=peer, device_id_type=MESH)
+
+    for step in reversed(steps[1:]):
+        greet((c, lax.rem(h + step, n_head)))
+    later = ((has_to[FAR], c + 4), (has_to[CROSS] & (core == 1), cross_to), (has_to[NEAR], c + 2))
+    earlier = (
+        (has_from[FAR], c - 4),
+        (has_from[CROSS] & (core == 0), cross_from),
+        (has_from[NEAR], c - 2),
+    )
+    for there, peer in later:
+        run_if(there, functools.partial(greet, (peer, h)))
+    greet((sibling, h))
+    n_later = sum(jnp.where(there, 1, 0) for there, _ in later)
+    n_earlier = sum(jnp.where(there, 1, 0) for there, _ in earlier)
+
     loads[0].start()
     loads[1].start()
-
-    barrier = pltpu.get_barrier_semaphore()
-
-    def greet(peer):
-        pl.semaphore_signal(barrier, inc=1, device_id=peer, device_id_type=MESH)
-
-    for step in range(1, n_head):
-        greet((c, lax.rem(h + step, n_head)))
-    greet((sibling, h))
-    n_peers = n_head
-    far_cross = jnp.where(core == 0, cross_from, cross_to)
-    for there, peer in (
-        (has_from[NEAR], c - 2),
-        (has_to[NEAR], c + 2),
-        (has_from[FAR], c - 4),
-        (has_to[FAR], c + 4),
-        ((far_cross >= 0) & (far_cross < n_ctx), far_cross),
-    ):
-
-        @pl.when(there)
-        def _(peer=peer):
-            greet((peer, h))
-
-        n_peers = n_peers + jnp.where(there, 1, 0)
-
     for load in loads[2:]:
         load.start()
     loads[0].wait()
@@ -163,7 +158,7 @@
         kv_stage[r, :piece] = k_in[:, cols]
         kv_stage[r, piece:] = v_in[:, cols]
     kv[OWN, slot_rows(0)] = kv_stage[h]
-    pl.semaphore_wait(barrier, n_peers)
+    pl.semaphore_wait(barrier, n_head + n_earlier)
 
     def send(src, dst, send_sem, recv_sem, to, sends=None, receives=None):
         copy = Message(src, dst, send_sem, recv_sem, to, sends, receives)
@@ -176,6 +171,12 @@
         y_copies[slot] = send(
             kv_stage.at[to], kv.at[OWN, slot_rows(slot)], y_send.at[slot], y_recv.at[slot], (c, to)
         )
+
+    def tell(peer):
+        pl.semaphore_signal(ready, inc=1, device_id=(peer, h), device_id_type=MESH)
+
+    for there, peer in earlier:
+        run_if(there, functools.partial(tell, peer))
 
     for role in (NEAR, FAR, CROSS):
 
@@ -217,6 +218,8 @@
     for group, slots in enumerate((range(1, near_slots), range(near_slots, n_head))):
         for slot in slots:
             y_copies[slot].wait_recv()
+        if group == 0:
+            run_if(n_later > 0, lambda: pl.semaphore_wait(ready, n_later))
         for role, to in ((FAR, c + 4), (CROSS, cross_to), (NEAR, c + 2)):
             send_on(OWN, role, to, group)
 
@@ -241,38 +244,49 @@
         both = both.reshape(n_head, 2, piece, d)
         return both[:, 0].reshape(tokens, d), both[:, 1].reshape(tokens, d)
 
-    def forward(role):
-        k_block, v_block = apart(kv[role])
-        cols = slice(role * tokens, (role + 1) * tokens)
-        k_cols[:, cols] = k_block.T
-        v_cols[:, cols] = v_block.T
-        visible = key_ids - back_by[role] * tokens >= starts
-        if role == OWN:
-            visible = visible & (key_ids <= query_ids)
+    def forward(*roles):
+        first, count = min(roles), len(roles)
+        blocks = [apart(kv[role]) for role in range(first, first + count)]
+        k_block = jnp.concatenate([block[0] for block in blocks], axis=0)
+        v_block = jnp.concatenate([block[1] for block in blocks], axis=0)
+        rows = slice(first * tokens, (first + count) * tokens)
+        k_cols[:, rows] = k_block.T
+        v_cols[:, rows] = v_block.T
         for j in range(chunks):
             qs = slice(j * chunk, (j + 1) * chunk)
-            scores = jnp.dot(k_block, q_cols[:, qs], preferred_element_type=F32)
-            scores = jnp.where(visible, scores, big_negative)
-            top = jnp.max(scores, axis=0, keepdims=True)
-            grown = jnp.exp2((scores - top) * (SCALE * LOG2E))
-            dp = jnp.dot(v_block, g_cols[:, qs], preferred_element_type=F32)
-            tops[role, j] = top
-            totals[role, j] = jnp.sum(grown, axis=0, keepdims=True)
-            deltas[role, j] = jnp.sum(grown * dp, axis=0, keepdims=True)
-            probs[cols, qs] = grown.astype(BF16)
-            dprobs[cols, qs] = dp
+            all_scores = jnp.dot(k_block, q_cols[:, qs], preferred_element_type=F32)
+            all_dp = jnp.dot(v_block, g_cols[:, qs], preferred_element_type=F32)
+            for i in range(count):
+                role = first + i
+                part_rows = slice(i * tokens, (i + 1) * tokens)
+                visible = key_ids - back_by[role] * tokens >= starts
+                if role == OWN:
+                    visible = visible & (key_ids <= query_ids)
+                scores = jnp.where(visible, all_scores[part_rows], big_negative)
+                top = jnp.max(scores, axis=0, keepdims=True)
+                grown = jnp.exp2((scores - top) * (SCALE * LOG2E))
+                dp = all_dp[part_rows]
+                tops[role, j] = top
+                totals[role, j] = jnp.sum(grown, axis=0, keepdims=True)
+                deltas[role, j] = jnp.sum(grown * dp, axis=0, keepdims=True)
+                cols = slice(role * tokens, (role + 1) * tokens)
+                probs[cols, qs] = grown.astype(BF16)
+                dprobs[cols, qs] = dp
 
     forward(OWN)
-    for group in range(2):
-        for role, there in ((NEAR, NEAR_SIB), (FAR, FAR_SIB)):
+    for role, there in ((NEAR, NEAR_SIB), (FAR, FAR_SIB)):
+        for group in range(2):
             c_copies[role, group].wait_recv()
             send_on(role, there, sibling, group)
-    forward(NEAR)
-    forward(FAR)
-    for role in (CROSS, NEAR_SIB, FAR_SIB):
+        if role == NEAR:
+            forward(NEAR)
+    for group in range(2):
+        c_copies[CROSS, group].wait_recv()
+    forward(FAR, CROSS)
+    for role in (NEAR_SIB, FAR_SIB):
         for group in range(2):
             c_copies[role, group].wait_recv()
-        forward(role)
+    forward(NEAR_SIB, FAR_SIB)
 
     factors, delta = {}, {}
     for j in range(chunks):
@@ -283,19 +297,29 @@
             factors[role, j] = lift[role] / total
         delta[j] = sum(factors[role, j] * deltas[role, j] for role in range(ROLES))
 
-    def backward(role):
-        rows = slice(role * tokens, (role + 1) * tokens)
+    def backward(*roles):
+        first, count = min(roles), len(roles)
         dk_part = dv_part = 0.0
         for j in range(chunks):
             qs = slice(j * chunk, (j + 1) * chunk)
-            p = probs[rows, qs].astype(F32) * factors[role, j]
-            ds = (p * (dprobs[rows, qs] - delta[j])).astype(BF16)
-            p = p.astype(BF16)
-            probs[rows, qs] = p
-            dscores[rows, qs] = ds
-            dk_part += jnp.dot(ds, by_rows(q_in, j), preferred_element_type=F32)
-            dv_part += jnp.dot(p, by_rows(g_in, j), preferred_element_type=F32)
-        return dk_part * SCALE, dv_part
+            ps, dss = [], []
+            for role in range(first, first + count):
+                rows = slice(role * tokens, (role + 1) * tokens)
+                p = probs[rows, qs].astype(F32) * factors[role, j]
+                ds = (p * (dprobs[rows, qs] - delta[j])).astype(BF16)
+                p = p.astype(BF16)
+                probs[rows, qs] = p
+                dscores[rows, qs] = ds
+                ps.append(p)
+                dss.append(ds)
+            dk_part += jnp.dot(
+                jnp.concatenate(dss, axis=0), by_rows(q_in, j), preferred_element_type=F32
+            )
+            dv_part += jnp.dot(
+                jnp.concatenate(ps, axis=0), by_rows(g_in, j), preferred_element_type=F32
+            )
+        cut = [slice(i * tokens, (i + 1) * tokens) for i in range(count)]
+        return {first + i: (dk_part[cut[i]] * SCALE, dv_part[cut[i]]) for i in range(count)}
 
     def by_rows(ref, j):
         pair = [
@@ -332,19 +356,19 @@
                 has_to.get(role),
             )
 
-    put(part.at[FAR_SIB], *backward(FAR_SIB))
-    send_back(FAR_SIB, sibling)
-    put(part.at[NEAR_SIB], *backward(NEAR_SIB))
-    send_back(NEAR_SIB, sibling)
-    put(part.at[CROSS], *backward(CROSS))
+    grads = backward(NEAR_SIB, FAR_SIB)
+    for role in (FAR_SIB, NEAR_SIB):
+        put(part.at[role], *grads[role])
+        send_back(role, sibling)
+    grads = backward(FAR, CROSS)
+    put(part.at[CROSS], *grads[CROSS])
     send_back(CROSS, cross_from)
-    far_grads = backward(FAR)
-    put(part.at[FAR], *with_back(FAR_SIB, *far_grads))
+    put(part.at[FAR], *with_back(FAR_SIB, *grads[FAR]))
     send_back(FAR, c - 4)
-    near_grads = backward(NEAR)
-    put(part.at[NEAR], *with_back(NEAR_SIB, *near_grads))
+    grads = backward(OWN, NEAR)
+    put(part.at[NEAR], *with_back(NEAR_SIB, *grads[NEAR]))
     send_back(NEAR, c - 2)
-    own_grads = backward(OWN)
+    own_grads = grads[OWN]
 
     for j in range(chunks):
         qs = slice(j * chunk, (j + 1) * chunk)
@@ -444,6 +468,7 @@
             dma((ROLES, 2)),
             dma((n_head,)),
             dma((n_head,)),
+            pltpu.SemaphoreType.REGULAR,
         ],
         compiler_params=pltpu.CompilerParams(
             collective_id=0, has_side_effects=True, vmem_limit_bytes=40 * 1024 * 1024

time: 34.2 us -> 33.1 us (0.968)
  Pallas kernels: 33.4 us -> 32.3 us
    pallas_call x1, Pallas kernels: 32.6 us -> 31.4 us  [per_device(): pl.pallas_call(functools.partial(kernel, n_ctx, n_head, tokens, heads), o...]
where the time goes in v4:
time: 33.1 us; the launch traced here: 33 us
  Pallas kernels  32.3 us (98%)
  between operations  0.64 us (2%)
    pallas_call x1, Pallas kernels, per_device(): pl.pallas_call(functools.partial(kernel, n_ctx, n_head, tokens, heads), o...  31.4 us
    pallas_call x1, Pallas kernels, per_device(): pl.pallas_call(write_out, out_shape=tuple((jax.ShapeDtypeStruct(x.shape,...  0.87 us

profile of v4, /device:TPU:198, one launch (start us, length us, event | category | flops | bytes accessed | tf_op | source)
XLA Modules:
  0.0 33.0 jit_solution(10304325079928974328)
XLA Ops:
  0.6 31.4 %shard_map.84 = (bf16[128,1024]{1,0:T(8,128)(2,1)S(1)}, bf16[128,1024]{1,0:T(8,128)(2,1)S(1)}, bf16[16,1024]{1,0:T(8,128)(2,1)S(1)}, bf16[16,1024]{1,0:T(8,128)(2,1)S(1)}) custom-call(bf16[128,1024]{1,0:T(8,128)(2,1)} %q_hbm.1, bf16[16,1024]{1,0:T(8,128)(2,1)} %k_hbm.1, bf16[16,1024]{1,0:T(8,128)(2,1)} %v_hbm.1, bf16[128,1024]{1,0:T(8,128)(2,1)} %g_hbm.1, ...), custom_call_target="tpu_custom_call" | custom-call | tf_op jit(solution)/shard_map/pallas_call | solution.py:433
  32.1 0.9 %shard_map.85 = (bf16[128,1024]{1,0:T(8,128)(2,1)}, bf16[128,1024]{1,0:T(8,128)(2,1)}, bf16[16,1024]{1,0:T(8,128)(2,1)}, bf16[16,1024]{1,0:T(8,128)(2,1)}) custom-call(bf16[128,1024]{1,0:T(8,128)(2,1)S(1)} %get-tuple-element.8.refs_0_, bf16[128,1024]{1,0:T(8,128)(2,1)S(1)} %get-tuple-element.9.refs_1_, bf16[16,1024]{1,0:T(8,128)(2,1)S(1)} %get-tuple-element.10.refs_2_, ...), custom_call_target="tpu_custom_call" | custom-call | tf_op jit(solution)/shard_map/pallas_call | solution.py:480

commit v5 on v4

--- a/solution.py
+++ b/solution.py
@@ -92,6 +92,7 @@
     back,
     grad_stage,
     grad_in,
+    far_in,
     in_sem,
     y_send,
     y_recv,
@@ -101,6 +102,8 @@
     b_recv,
     z_send,
     z_recv,
+    f_send,
+    f_recv,
     ready,
 ):
     d = HEAD_SIZE
@@ -111,6 +114,7 @@
     width = heads * tokens
     steps = ring_steps(n_head)
     near_slots = n_head // 2 + 1
+    back_slots = n_head - 5
     groups = (pl.ds(0, near_slots * 2 * piece), pl.ds(near_slots * 2 * piece, (n_head - near_slots) * 2 * piece))
 
     def slot_rows(slot):
@@ -187,6 +191,7 @@
         @pl.when(jnp.logical_not(has_to[role]))
         def _(role=role):
             back[role] = jnp.zeros(back.shape[1:], BF16)
+            far_in[role] = jnp.zeros(far_in.shape[1:], BF16)
 
     loads[2].wait()
     ids_row = lax.broadcasted_iota(jnp.int32, (128, 128), 0)
@@ -336,38 +341,53 @@
         where[...] = together(dk_part, dv_part, BF16)
 
     def with_back(role, dk_part, dv_part):
-        for group in range(2):
-            b_copies[role, group].wait_recv()
+        b_copies[role].wait_recv()
         dk_back, dv_back = apart(back[role])
         return dk_part + dk_back.astype(F32), dv_part + dv_back.astype(F32)
 
-    b_copies = {}
-
-    def send_back(role, to):
-        for group in (1, 0):
-            rows = groups[group]
-            b_copies[role, group] = send(
-                part.at[role, rows],
-                back.at[role, rows],
-                b_send.at[role, group],
-                b_recv.at[role, group],
-                (to, h),
+    b_copies, f_copies = {}, {}
+
+    def send_back(role, to, rows):
+        b_copies[role] = send(
+            part.at[role, rows],
+            back.at[role, rows],
+            b_send.at[role],
+            b_recv.at[role],
+            (to, h),
+            has_from.get(role),
+            has_to.get(role),
+        )
+
+    def send_far(role, to):
+        for slot in reversed(range(back_slots, n_head)):
+            f_copies[role, slot] = send(
+                part.at[role, slot_rows(slot)],
+                far_in.at[role, slot],
+                f_send.at[role, slot],
+                f_recv.at[role, slot],
+                (to, lax.rem(h + steps[slot], n_head)),
                 has_from.get(role),
                 has_to.get(role),
             )
 
+    whole = pl.ds(0, 2 * tokens)
     grads = backward(NEAR_SIB, FAR_SIB)
     for role in (FAR_SIB, NEAR_SIB):
         put(part.at[role], *grads[role])
-        send_back(role, sibling)
+        send_back(role, sibling, whole)
     grads = backward(FAR, CROSS)
     put(part.at[CROSS], *grads[CROSS])
-    send_back(CROSS, cross_from)
+    send_far(CROSS, cross_from)
+    send_back(CROSS, cross_from, pl.ds(0, back_slots * 2 * piece))
     put(part.at[FAR], *with_back(FAR_SIB, *grads[FAR]))
-    send_back(FAR, c - 4)
+    send_far(FAR, c - 4)
+    send_back(FAR, c - 4, pl.ds(0, back_slots * 2 * piece))
     grads = backward(OWN, NEAR)
     put(part.at[NEAR], *with_back(NEAR_SIB, *grads[NEAR]))
-    send_back(NEAR, c - 2)
+    send_far(NEAR, c - 2)
+    send_back(NEAR, c - 2, pl.ds(0, back_slots * 2 * piece))
+    put(part.at[OWN], *grads[OWN])
+    send_far(OWN, c)
     own_grads = grads[OWN]
 
     for j in range(chunks):
@@ -381,36 +401,42 @@
             dq[:, r * d : (r + 1) * d] = grad[:, i * tokens : (i + 1) * tokens].T
     for copy in list(y_copies.values()) + list(c_copies.values()):
         copy.wait_send()
-    own_sum = together(*own_grads, F32)
+    rows = slice(0, back_slots * 2 * piece)
+    total = together(*own_grads, F32)[rows]
+    for role in (CROSS, FAR, NEAR):
+        b_copies[role].wait_recv()
+        total += back[role, rows].astype(F32)
+    grad_stage[rows] = total.astype(BF16)
     z_copies = {}
-    for group, slots in ((1, range(near_slots, n_head)), (0, range(near_slots))):
-        rows = slice(groups[group].start, groups[group].start + groups[group].size)
-        for role in (CROSS, FAR, NEAR):
-            b_copies[role, group].wait_recv()
-        total = own_sum[rows]
-        for role in (CROSS, FAR, NEAR):
-            total += back[role, rows].astype(F32)
-        grad_stage[rows] = total.astype(BF16)
-        for slot in reversed(slots):
-            if slot:
-                to = lax.rem(h + steps[slot], n_head)
-                z_copies[slot] = send(
-                    grad_stage.at[slot_rows(slot)],
-                    grad_in.at[h],
-                    z_send.at[slot],
-                    z_recv.at[slot],
-                    (c, to),
-                )
-    grad_in[h] = grad_stage[slot_rows(0)]
+    for slot in reversed(range(1, back_slots)):
+        z_copies[slot] = send(
+            grad_stage.at[slot_rows(slot)],
+            grad_in.at[slot],
+            z_send.at[slot],
+            z_recv.at[slot],
+            (c, lax.rem(h + steps[slot], n_head)),
+        )
+
+    def finish(slot, both):
+        owner = lax.rem(h + n_head - steps[slot], n_head)
+        cols = pl.ds(pl.multiple_of(owner * d, d), d)
+        dk_out[:, cols] = both[:piece]
+        dv_out[:, cols] = both[piece:]
+
+    finish(0, grad_stage[slot_rows(0)])
     for copy in b_copies.values():
         copy.wait_send()
-    for copy in z_copies.values():
-        copy.wait_recv()
-    for r in range(n_head):
-        dk_out[:, r * d : (r + 1) * d] = grad_in[r, :piece]
-        dv_out[:, r * d : (r + 1) * d] = grad_in[r, piece:]
-
-    for copy in z_copies.values():
+    for slot in range(back_slots, n_head):
+        total = 0.0
+        for role in (OWN, CROSS, FAR, NEAR):
+            f_copies[role, slot].wait_recv()
+            total += far_in[role, slot].astype(F32)
+        finish(slot, total.astype(BF16))
+    for slot in range(1, back_slots):
+        z_copies[slot].wait_recv()
+        finish(slot, grad_in[slot])
+
+    for copy in list(f_copies.values()) + list(z_copies.values()):
         copy.wait_send()
 
 
@@ -459,15 +485,18 @@
             pltpu.VMEM((ROLES, *block), BF16),
             pltpu.VMEM(block, BF16),
             pltpu.VMEM((n_head, 2 * piece, d), BF16),
+            pltpu.VMEM((4, n_head, 2 * piece, d), BF16),
             dma((5,)),
             dma((n_head,)),
             dma((n_head,)),
             dma((ROLES, 2)),
             dma((ROLES, 2)),
-            dma((ROLES, 2)),
-            dma((ROLES, 2)),
+            dma((ROLES,)),
+            dma((ROLES,)),
             dma((n_head,)),
             dma((n_head,)),
+            dma((4, n_head)),
+            dma((4, n_head)),
             pltpu.SemaphoreType.REGULAR,
         ],
         compiler_params=pltpu.CompilerParams(

time: 33.1 us -> 31.9 us (0.964)
  Pallas kernels: 32.3 us -> 30.9 us
    pallas_call x1, Pallas kernels: 31.4 us -> 30 us  [per_device(): pl.pallas_call(functools.partial(kernel, n_ctx, n_head, tokens, heads), o...]
where the time goes in v5:
time: 31.9 us; the launch traced here: 31.6 us
  Pallas kernels  30.9 us (97%)
  between operations  0.64 us (2%)
    pallas_call x1, Pallas kernels, per_device(): pl.pallas_call(functools.partial(kernel, n_ctx, n_head, tokens, heads), o...  30 us
    pallas_call x1, Pallas kernels, per_device(): pl.pallas_call(write_out, out_shape=tuple((jax.ShapeDtypeStruct(x.shape,...  0.87 us

profile of v5, /device:TPU:198, one launch (start us, length us, event | category | flops | bytes accessed | tf_op | source)
XLA Modules:
  0.0 31.6 jit_solution(17251317445565806758)
XLA Ops:
  0.6 30.0 %shard_map.84 = (bf16[128,1024]{1,0:T(8,128)(2,1)S(1)}, bf16[128,1024]{1,0:T(8,128)(2,1)S(1)}, bf16[16,1024]{1,0:T(8,128)(2,1)S(1)}, bf16[16,1024]{1,0:T(8,128)(2,1)S(1)}) custom-call(bf16[128,1024]{1,0:T(8,128)(2,1)} %q_hbm.1, bf16[16,1024]{1,0:T(8,128)(2,1)} %k_hbm.1, bf16[16,1024]{1,0:T(8,128)(2,1)} %v_hbm.1, bf16[128,1024]{1,0:T(8,128)(2,1)} %g_hbm.1, ...), custom_call_target="tpu_custom_call" | custom-call | tf_op jit(solution)/shard_map/pallas_call | solution.py:459
  30.7 0.9 %shard_map.85 = (bf16[128,1024]{1,0:T(8,128)(2,1)}, bf16[128,1024]{1,0:T(8,128)(2,1)}, bf16[16,1024]{1,0:T(8,128)(2,1)}, bf16[16,1024]{1,0:T(8,128)(2,1)}) custom-call(bf16[128,1024]{1,0:T(8,128)(2,1)S(1)} %get-tuple-element.8.refs_0_, bf16[128,1024]{1,0:T(8,128)(2,1)S(1)} %get-tuple-element.9.refs_1_, bf16[16,1024]{1,0:T(8,128)(2,1)S(1)} %get-tuple-element.10.refs_2_, ...), custom_call_target="tpu_custom_call" | custom-call | tf_op jit(solution)/shard_map/pallas_call | solution.py:509

commit v6 on v5

--- a/solution.py
+++ b/solution.py
@@ -113,7 +113,7 @@
     piece = tokens // n_head
     width = heads * tokens
     steps = ring_steps(n_head)
-    near_slots = n_head // 2 + 1
+    near_slots = 3
     back_slots = n_head - 5
     groups = (pl.ds(0, near_slots * 2 * piece), pl.ds(near_slots * 2 * piece, (n_head - near_slots) * 2 * piece))
 
@@ -282,15 +282,16 @@
     for role, there in ((NEAR, NEAR_SIB), (FAR, FAR_SIB)):
         for group in range(2):
             c_copies[role, group].wait_recv()
-            send_on(role, there, sibling, group)
+        c_copies[there] = send(
+            kv.at[role], kv.at[there], c_send.at[there, 0], c_recv.at[there, 0], (sibling, h)
+        )
         if role == NEAR:
             forward(NEAR)
     for group in range(2):
         c_copies[CROSS, group].wait_recv()
     forward(FAR, CROSS)
     for role in (NEAR_SIB, FAR_SIB):
-        for group in range(2):
-            c_copies[role, group].wait_recv()
+        c_copies[role].wait_recv()
     forward(NEAR_SIB, FAR_SIB)
 
     factors, delta = {}, {}

time: 31.9 us -> 31.8 us (level)
  no operation moved by 1% of the time
where the time goes in v6:
time: 31.8 us; the launch traced here: 31.6 us
  Pallas kernels  31 us (97%)
  between operations  0.64 us (2%)
    pallas_call x1, Pallas kernels, per_device(): pl.pallas_call(functools.partial(kernel, n_ctx, n_head, tokens, heads), o...  30.1 us
    pallas_call x1, Pallas kernels, per_device(): pl.pallas_call(write_out, out_shape=tuple((jax.ShapeDtypeStruct(x.shape,...  0.87 us

profile of v6, /device:TPU:198, one launch (start us, length us, event | category | flops | bytes accessed | tf_op | source)
XLA Modules:
  0.0 31.6 jit_solution(14132612482756667367)
XLA Ops:
  0.6 30.1 %shard_map.84 = (bf16[128,1024]{1,0:T(8,128)(2,1)S(1)}, bf16[128,1024]{1,0:T(8,128)(2,1)S(1)}, bf16[16,1024]{1,0:T(8,128)(2,1)S(1)}, bf16[16,1024]{1,0:T(8,128)(2,1)S(1)}) custom-call(bf16[128,1024]{1,0:T(8,128)(2,1)} %q_hbm.1, bf16[16,1024]{1,0:T(8,128)(2,1)} %k_hbm.1, bf16[16,1024]{1,0:T(8,128)(2,1)} %v_hbm.1, bf16[128,1024]{1,0:T(8,128)(2,1)} %g_hbm.1, ...), custom_call_target="tpu_custom_call" | custom-call | tf_op jit(solution)/shard_map/pallas_call | solution.py:460
  30.8 0.9 %shard_map.85 = (bf16[128,1024]{1,0:T(8,128)(2,1)}, bf16[128,1024]{1,0:T(8,128)(2,1)}, bf16[16,1024]{1,0:T(8,128)(2,1)}, bf16[16,1024]{1,0:T(8,128)(2,1)}) custom-call(bf16[128,1024]{1,0:T(8,128)(2,1)S(1)} %get-tuple-element.8.refs_0_, bf16[128,1024]{1,0:T(8,128)(2,1)S(1)} %get-tuple-element.9.refs_1_, bf16[16,1024]{1,0:T(8,128)(2,1)S(1)} %get-tuple-element.10.refs_2_, ...), custom_call_target="tpu_custom_call" | custom-call | tf_op jit(solution)/shard_map/pallas_call | solution.py:510
